TPU v7x, 256 devices: a whole 4x4x8 slice. The times are simulated.
256 devices in a mesh: gx: 4 (over x), gyz: 32 (over z, y), band: 2 (over core).
Axes of the slice: x: 4, y: 4, z: 8, core: 2. Of those that a mesh axis runs over, the one named last changes fastest.
Arguments:
- block: float32 [16, 16, 256, 128], P('band', 'gx', 'gyz'), may hold values from -6 to 6
- potential: float32 [16, 256, 128], P('gx', 'gyz'), may hold values from -1 to 1
- proj_index: int32 [1024, 128], P(('gx', 'gyz')), may hold values from 0 to 4095
- proj_value: float32 [1024, 128], P(('gx', 'gyz')), may hold values from -0.5 to 0.5
- proj_strength: float32 [1024], P(('gx', 'gyz')), may hold values from 0.5 to 2
- stored: float32 [1024, 16, 256, 128], P('band', 'gx', 'gyz'), may hold values from -0.0078125 to 0.0078125
Outputs:
- projected: float32 [16, 16, 256, 128], P('band', 'gx', 'gyz')
- intersection: float32 [1024, 16], P('band')
Inputs may be any that keep to these rules, and one draw needn't show every extreme that they name: `proj_index`: flat index of a cell within the grid block of 4 x 8 x 128 cells that holds the projector, z fastest; cells of one projector may repeat.
All inputs are finite; a program needn't handle non-finite values.
Results may differ from a plain program's by a relative error of at most 0.00008.
Values sent between devices are 32-bit elements; how exact they have to be, the bound alone decides.
A program may use at most 64 MiB of HBM per device.

v0:
```python
from functools import partial

import jax
import jax.numpy as jnp
from jax import lax
from jax.sharding import PartitionSpec as P

DEGREE = 8


LOW_EDGE = 0.0
CUT_EDGE = 1.0
TOP_EDGE = 10.0


def extended(cells, sides, width):
    for axis, dim in sides:
        count = lax.axis_size(axis)
        head = lax.slice_in_dim(cells, 0, width, axis=dim)
        tail = lax.slice_in_dim(cells, cells.shape[dim] - width, cells.shape[dim], axis=dim)
        cells = jnp.concatenate(
            [
                lax.ppermute(tail, axis, [(i, (i + 1) % count) for i in range(count)]),
                cells,
                lax.ppermute(head, axis, [((i + 1) % count, i) for i in range(count)]),
            ],
            axis=dim,
        )
    return cells


def chebyshev(start_block, hamiltonian):
    half_width = (TOP_EDGE - CUT_EDGE) / 2.0
    center = (TOP_EDGE + CUT_EDGE) / 2.0
    sigma_first = half_width / (LOW_EDGE - center)
    previous = start_block
    current = sigma_first / half_width * (hamiltonian(start_block) - center * start_block)
    sigma_now = sigma_first
    for turn_index in range(DEGREE - 1):
        sigma_next = 1.0 / (2.0 / sigma_first - sigma_now)
        following = (
            2.0 * sigma_next / half_width * (hamiltonian(current) - center * current)
            - sigma_now * sigma_next * previous
        )
        previous, current, sigma_now = (current, following, sigma_next)
    return current


def nonlocal_term(flat_block, cell_index, proj_value, proj_strength):
    picked = flat_block[:, cell_index]
    weights = jnp.sum(picked * proj_value[None], axis=2) * proj_strength[None]
    spread = weights[:, :, None] * proj_value[None]
    return jnp.zeros_like(flat_block).at[:, cell_index].add(spread)


def hamiltonian_local(field, potential, cell_index, proj_value, proj_strength):
    padded = extended(field, (("gx", 1), ("gyz", 2)), 1)
    neighbours = (
        padded[:, 2:, 1:-1] + padded[:, :-2, 1:-1] + padded[:, 1:-1, 2:] + padded[:, 1:-1, :-2]
    )
    zpadded = jnp.pad(field, ((0, 0), (0, 0), (0, 0), (1, 1)))
    neighbours = neighbours + zpadded[..., 2:] + zpadded[..., :-2]
    local_part = -0.5 * (neighbours - 6.0 * field) + potential[None] * field
    count = field.shape[0]
    flat = field.reshape(count, -1)
    return local_part + nonlocal_term(flat, cell_index, proj_value, proj_strength).reshape(
        field.shape
    )


def on_device(block, potential, proj_index, proj_value, proj_strength, stored):
    hamiltonian = partial(
        hamiltonian_local,
        potential=potential,
        cell_index=proj_index,
        proj_value=proj_value,
        proj_strength=proj_strength,
    )
    own_rows = block.shape[0]
    own_filtered = chebyshev(block, hamiltonian)
    filtered = lax.all_gather(own_filtered, "band", axis=0, tiled=True)
    flat_filtered = filtered.reshape(filtered.shape[0], -1)
    flat_stored = stored.reshape(stored.shape[0], -1)
    partial_intersection = jnp.dot(flat_stored, flat_filtered.T, precision=lax.Precision.HIGHEST)
    intersection = lax.psum(partial_intersection, ("gx", "gyz"))
    correction = lax.psum_scatter(
        jnp.dot(intersection.T, flat_stored, precision=lax.Precision.HIGHEST),
        "band",
        scatter_dimension=0,
        tiled=True,
    )
    projected = (own_filtered.reshape(own_rows, -1) - correction).reshape(own_filtered.shape)
    return (projected, intersection)


def solution(mesh):
    in_specs = (
        P("band", "gx", "gyz", None),
        P("gx", "gyz", None),
        P(("gx", "gyz"), None),
        P(("gx", "gyz"), None),
        P(("gx", "gyz")),
        P("band", "gx", "gyz", None),
    )
    out_specs = (P("band", "gx", "gyz", None), P("band", None))
    return jax.shard_map(
        on_device, mesh=mesh, in_specs=in_specs, out_specs=out_specs, check_vma=False
    )
```

profile of v0, /device:TPU:1, one launch (start us, length us, event | category | flops | bytes accessed | tf_op | source)
XLA Modules:
  0.0 913.4 jit_solution(4880485963396761105)
XLA Ops:
  13.3 2.8 gather_fusion
  18.3 6.8 collective-permute-start.2
  25.1 6.5 scatter_custom_fusion
  33.0 2.8 gather_fusion.1
  41.4 5.0 collective-permute-start.6
  46.6 6.5 scatter_custom_fusion.1
  54.5 2.8 gather_fusion.2
  61.7 4.8 collective-permute-start.10
  66.7 6.7 scatter_custom_fusion.2
  81.9 5.3 collective-permute-start.14
  87.4 6.7 scatter_custom_fusion.3
  102.6 4.8 collective-permute-start.18
  107.6 6.7 scatter_custom_fusion.4
  122.9 4.8 collective-permute-start.22
  127.9 6.7 scatter_custom_fusion.5
  143.1 4.8 collective-permute-start.26
  148.1 6.7 scatter_custom_fusion.6
  163.5 4.8 collective-permute-start.30
  168.5 6.7 scatter_custom_fusion.7
  175.9 16.1 %all_gather.3 = f32[16,4,8,128]{3,0,2,1:T(8,128)S(1)} all-gather(f32[8,4,8,128]{3,0,2,1:T(8,128)S(1)} %fusion.93), channel_id=1, replica_groups=mesh['gx'=4,'gyz'=32,'band'=2] {'band'}, dimensions={0}, use_global_device_ids=true | all-gather | bytes 393216 | tf_op jit(solution)/shard_map/all_gather | solution.py:81
  192.0 13.7 %fusion.5 = f32[512,16]{0,1:T(8,128)S(1)} fusion(f32[16,4,8,128]{3,0,2,1:T(8,128)S(1)} %all_gather.3, f32[512,4,8,128]{3,2,1,0:T(8,128)} %param.11), kind=kOutput, calls=%fused_computation.21 | convolution fusion | flops 402653184 | bytes 8683520 | tf_op jit(solution)/shard_map/dot_general | solution.py:84
  205.6 571.5 %psum.7 = f32[512,16]{0,1:T(8,128)S(1)} all-reduce(f32[512,16]{0,1:T(8,128)S(1)} %fusion.5), channel_id=1, replica_groups=mesh['gx'=4,'gyz'=32,'band'=2] {'gx','gyz'}, use_global_device_ids=true, to_apply=%region_16.17 | all-reduce | flops 8192 | bytes 65536 | tf_op jit(solution)/shard_map/psum | solution.py:85
  777.1 12.7 %fusion = f32[16,4096]{1,0:T(8,128)} fusion(f32[512,16]{0,1:T(8,128)S(1)} %psum.7, f32[64,8,32,128]{3,2,1,0:T(8,128)} %bitcast.91), kind=kOutput, calls=%fused_computation.16 | convolution fusion | flops 402653184 | bytes 8683520 | tf_op jit(solution)/shard_map/dot_general | solution.py:87
  789.9 114.7 %reduce-scatter.2.cloned.1.call-done = f32[8,4096]{1,0:T(8,128)} async-done(((f32[16,4096]{1,0:T(8,128)}), f32[8,4096]{1,0:T(8,128)}) %reduce-scatter.2.cloned.1.call-update) | async-done | bytes 131088 | tf_op jit(solution)/shard_map/reduce_scatter | solution.py:86
  (150 shorter events, 67.3 us)
Async XLA Ops:
  7.2 897.3 %reduce-scatter.2.cloned.1.call-start = ((), (), s32[]{:S(2)}) async-start(), calls=%async_computation.1 | async-start | bytes 393216 | tf_op jit(solution)/shard_map/reduce_scatter | solution.py:86
  8.3 8.4 collective-permute-start.1
  10.4 6.4 collective-permute-start
  16.8 15.4 %collective-permute-start.3 = (f32[8,6,1,128]{3,0,2,1:T(8,128)S(1)}, f32[8,6,1,128]{3,0,2,1:T(8,128)S(1)}, u32[]{:S(2)}, u32[]{:S(2)}) collective-permute-start(f32[8,6,1,128]{3,0,2,1:T(8,128)S(1)} %get-tuple-element.23), channel_id=1, source_target_pairs={{0,2},{2,4},{4,6},{6,8},{8,10},{10,12},{12,14},{14,16},{16,18},{18... | collective-permute-start | bytes 73736 | tf_op jit(solution)/shard_map/ppermute | solution.py:23
  18.3 13.9 %collective-permute-start.2 = (f32[8,6,1,128]{3,0,2,1:T(8,128)S(1)}, f32[8,6,1,128]{3,0,2,1:T(8,128)S(1)}, u32[]{:S(2)}, u32[]{:S(2)}) collective-permute-start(f32[8,6,1,128]{3,0,2,1:T(8,128)S(1)} %get-tuple-element.22), channel_id=1, source_target_pairs={{2,0},{4,2},{6,4},{8,6},{10,8},{12,10},{14,12},{16,14},{18,16},{20... | collective-permute-start | bytes 73736 | tf_op jit(solution)/shard_map/ppermute | solution.py:25
  41.4 12.3 %collective-permute-start.7 = (f32[8,6,1,128]{3,0,2,1:T(8,128)S(1)}, f32[8,6,1,128]{3,0,2,1:T(8,128)S(1)}, u32[]{:S(2)}, u32[]{:S(2)}) collective-permute-start(f32[8,6,1,128]{3,0,2,1:T(8,128)S(1)} %get-tuple-element.21), channel_id=1, source_target_pairs={{0,2},{2,4},{4,6},{6,8},{8,10},{10,12},{12,14},{14,16},{16,18},{18... | collective-permute-start | bytes 73736 | tf_op jit(solution)/shard_map/ppermute | solution.py:23
  41.4 12.3 %collective-permute-start.6 = (f32[8,6,1,128]{3,0,2,1:T(8,128)S(1)}, f32[8,6,1,128]{3,0,2,1:T(8,128)S(1)}, u32[]{:S(2)}, u32[]{:S(2)}) collective-permute-start(f32[8,6,1,128]{3,0,2,1:T(8,128)S(1)} %get-tuple-element.20), channel_id=1, source_target_pairs={{2,0},{4,2},{6,4},{8,6},{10,8},{12,10},{14,12},{16,14},{18,16},{20... | collective-permute-start | bytes 73736 | tf_op jit(solution)/shard_map/ppermute | solution.py:25
  61.7 12.2 %collective-permute-start.11 = (f32[8,6,1,128]{3,0,2,1:T(8,128)S(1)}, f32[8,6,1,128]{3,0,2,1:T(8,128)S(1)}, u32[]{:S(2)}, u32[]{:S(2)}) collective-permute-start(f32[8,6,1,128]{3,0,2,1:T(8,128)S(1)} %get-tuple-element.19), channel_id=1, source_target_pairs={{0,2},{2,4},{4,6},{6,8},{8,10},{10,12},{12,14},{14,16},{16,18},{18... | collective-permute-start | bytes 73736 | tf_op jit(solution)/shard_map/ppermute | solution.py:23
  61.7 12.2 %collective-permute-start.10 = (f32[8,6,1,128]{3,0,2,1:T(8,128)S(1)}, f32[8,6,1,128]{3,0,2,1:T(8,128)S(1)}, u32[]{:S(2)}, u32[]{:S(2)}) collective-permute-start(f32[8,6,1,128]{3,0,2,1:T(8,128)S(1)} %get-tuple-element.18), channel_id=1, source_target_pairs={{2,0},{4,2},{6,4},{8,6},{10,8},{12,10},{14,12},{16,14},{18,16},{20... | collective-permute-start | bytes 73736 | tf_op jit(solution)/shard_map/ppermute | solution.py:25
  77.9 4.0 collective-permute-start.13
  81.9 12.7 %collective-permute-start.15 = (f32[8,6,1,128]{3,0,2,1:T(8,128)S(1)}, f32[8,6,1,128]{3,0,2,1:T(8,128)S(1)}, u32[]{:S(2)}, u32[]{:S(2)}) collective-permute-start(f32[8,6,1,128]{3,0,2,1:T(8,128)S(1)} %get-tuple-element.17), channel_id=1, source_target_pairs={{0,2},{2,4},{4,6},{6,8},{8,10},{10,12},{12,14},{14,16},{16,18},{18... | collective-permute-start | bytes 73736 | tf_op jit(solution)/shard_map/ppermute | solution.py:23
  81.9 12.7 %collective-permute-start.14 = (f32[8,6,1,128]{3,0,2,1:T(8,128)S(1)}, f32[8,6,1,128]{3,0,2,1:T(8,128)S(1)}, u32[]{:S(2)}, u32[]{:S(2)}) collective-permute-start(f32[8,6,1,128]{3,0,2,1:T(8,128)S(1)} %get-tuple-element.16), channel_id=1, source_target_pairs={{2,0},{4,2},{6,4},{8,6},{10,8},{12,10},{14,12},{16,14},{18,16},{20... | collective-permute-start | bytes 73736 | tf_op jit(solution)/shard_map/ppermute | solution.py:25
  98.6 4.0 collective-permute-start.17
  102.6 12.2 %collective-permute-start.19 = (f32[8,6,1,128]{3,0,2,1:T(8,128)S(1)}, f32[8,6,1,128]{3,0,2,1:T(8,128)S(1)}, u32[]{:S(2)}, u32[]{:S(2)}) collective-permute-start(f32[8,6,1,128]{3,0,2,1:T(8,128)S(1)} %get-tuple-element.15), channel_id=1, source_target_pairs={{0,2},{2,4},{4,6},{6,8},{8,10},{10,12},{12,14},{14,16},{16,18},{18... | collective-permute-start | bytes 73736 | tf_op jit(solution)/shard_map/ppermute | solution.py:23
  102.6 12.2 %collective-permute-start.18 = (f32[8,6,1,128]{3,0,2,1:T(8,128)S(1)}, f32[8,6,1,128]{3,0,2,1:T(8,128)S(1)}, u32[]{:S(2)}, u32[]{:S(2)}) collective-permute-start(f32[8,6,1,128]{3,0,2,1:T(8,128)S(1)} %get-tuple-element.14), channel_id=1, source_target_pairs={{2,0},{4,2},{6,4},{8,6},{10,8},{12,10},{14,12},{16,14},{18,16},{20... | collective-permute-start | bytes 73736 | tf_op jit(solution)/shard_map/ppermute | solution.py:25
  118.8 4.0 collective-permute-start.21
  122.8 12.4 %collective-permute-start.23 = (f32[8,6,1,128]{3,0,2,1:T(8,128)S(1)}, f32[8,6,1,128]{3,0,2,1:T(8,128)S(1)}, u32[]{:S(2)}, u32[]{:S(2)}) collective-permute-start(f32[8,6,1,128]{3,0,2,1:T(8,128)S(1)} %get-tuple-element.13), channel_id=1, source_target_pairs={{0,2},{2,4},{4,6},{6,8},{8,10},{10,12},{12,14},{14,16},{16,18},{18... | collective-permute-start | bytes 73736 | tf_op jit(solution)/shard_map/ppermute | solution.py:23
  122.9 12.2 %collective-permute-start.22 = (f32[8,6,1,128]{3,0,2,1:T(8,128)S(1)}, f32[8,6,1,128]{3,0,2,1:T(8,128)S(1)}, u32[]{:S(2)}, u32[]{:S(2)}) collective-permute-start(f32[8,6,1,128]{3,0,2,1:T(8,128)S(1)} %get-tuple-element.12), channel_id=1, source_target_pairs={{2,0},{4,2},{6,4},{8,6},{10,8},{12,10},{14,12},{16,14},{18,16},{20... | collective-permute-start | bytes 73736 | tf_op jit(solution)/shard_map/ppermute | solution.py:25
  139.1 4.0 collective-permute-start.25
  143.1 12.2 %collective-permute-start.27 = (f32[8,6,1,128]{3,0,2,1:T(8,128)S(1)}, f32[8,6,1,128]{3,0,2,1:T(8,128)S(1)}, u32[]{:S(2)}, u32[]{:S(2)}) collective-permute-start(f32[8,6,1,128]{3,0,2,1:T(8,128)S(1)} %get-tuple-element.11), channel_id=1, source_target_pairs={{0,2},{2,4},{4,6},{6,8},{8,10},{10,12},{12,14},{14,16},{16,18},{18... | collective-permute-start | bytes 73736 | tf_op jit(solution)/shard_map/ppermute | solution.py:23
  143.1 12.2 %collective-permute-start.26 = (f32[8,6,1,128]{3,0,2,1:T(8,128)S(1)}, f32[8,6,1,128]{3,0,2,1:T(8,128)S(1)}, u32[]{:S(2)}, u32[]{:S(2)}) collective-permute-start(f32[8,6,1,128]{3,0,2,1:T(8,128)S(1)} %get-tuple-element.10), channel_id=1, source_target_pairs={{2,0},{4,2},{6,4},{8,6},{10,8},{12,10},{14,12},{16,14},{18,16},{20... | collective-permute-start | bytes 73736 | tf_op jit(solution)/shard_map/ppermute | solution.py:25
  159.3 4.0 collective-permute-start.29
  163.3 12.4 %collective-permute-start.31 = (f32[8,6,1,128]{3,0,2,1:T(8,128)S(1)}, f32[8,6,1,128]{3,0,2,1:T(8,128)S(1)}, u32[]{:S(2)}, u32[]{:S(2)}) collective-permute-start(f32[8,6,1,128]{3,0,2,1:T(8,128)S(1)} %get-tuple-element.9), channel_id=1, source_target_pairs={{0,2},{2,4},{4,6},{6,8},{8,10},{10,12},{12,14},{14,16},{16,18},{18... | collective-permute-start | bytes 73736 | tf_op jit(solution)/shard_map/ppermute | solution.py:23
  163.5 12.2 %collective-permute-start.30 = (f32[8,6,1,128]{3,0,2,1:T(8,128)S(1)}, f32[8,6,1,128]{3,0,2,1:T(8,128)S(1)}, u32[]{:S(2)}, u32[]{:S(2)}) collective-permute-start(f32[8,6,1,128]{3,0,2,1:T(8,128)S(1)} %get-tuple-element.8), channel_id=1, source_target_pairs={{2,0},{4,2},{6,4},{8,6},{10,8},{12,10},{14,12},{16,14},{18,16},{20... | collective-permute-start | bytes 73736 | tf_op jit(solution)/shard_map/ppermute | solution.py:25
  (16 other events, 105.2 us)
Sparse Core Ops, SparseCore 0:
  790.0 114.4 reduce-scatter.1
where the time goes:
time: 921 us; the launch traced here: 913 us
  blocking collectives  588 us (64%)
  waiting for transfers between devices  134 us (15%)
  other arithmetic  59 us (6%)
  starting transfers between devices  57.1 us (6%)
  local copies, waits for them, and re-layouts  34.6 us (4%)
  matrix products  26.4 us (3%)
  between operations  15.1 us (2%)
    psum x1, blocking collectives, on_device(): intersection = lax.psum(partial_intersection, ('gx', 'gyz'))  571 us
    reduce_scatter x1, waiting for transfers between devices, on_device(): lax.psum_scatter(jnp.dot(intersection.T, flat_stored, precision=lax.Preci...  115 us
    scatter-add x8, other arithmetic, nonlocal_term(): return jnp.zeros_like(flat_block).at[:, cell_index].add(spread)  53 us
    ppermute x16, starting transfers between devices, extended(): lax.ppermute(head, axis, [((i + 1) % count, i) for i in range(count)])  44.6 us
    gather x8, local copies, waits for them, and re-layouts, nonlocal_term(): picked = flat_block[:, cell_index]  22.5 us
  transfers between devices with their start and end apart: 33, of which 15 were waited for; matrix products, arithmetic and copies ran while one was open for 7% of the time, Pallas kernels for 0%

commit v1 on v0

v1 whole, which is shorter than its diff:
```python
import functools

import jax
import jax.numpy as jnp
from jax import lax
from jax.experimental import pallas as pl
from jax.experimental.pallas import tpu as pltpu
from jax.sharding import PartitionSpec as P

DEGREE = 8
LOW_EDGE = 0.0
CUT_EDGE = 1.0
TOP_EDGE = 10.0
HALF = (TOP_EDGE - CUT_EDGE) / 2.0
CENTER = (TOP_EDGE + CUT_EDGE) / 2.0

MESH = pl.DeviceIdType.MESH
F32 = jnp.float32
BF16 = jnp.bfloat16

CX, CY, CZ = 4, 8, 128
NXY = CX * CY
CELLS = NXY * CZ
ORB = 8
NPROJ = 8
NJ = 512
NG_X, NG_Y, NG_Z = 4, 4, 8
PLANE = NG_X * NG_Y


def recurrence():
    first = HALF / (LOW_EDGE - CENTER)
    scales, backs = [first / HALF], [0.0]
    now = first
    for _ in range(DEGREE - 1):
        after = 1.0 / (2.0 / first - now)
        scales.append(2.0 * after / HALF)
        backs.append(now * after)
        now = after
    return scales, backs


SCALES, BACKS = recurrence()


def pick(k, values):
    out = jnp.float32(values[-1])
    for i in range(len(values) - 2, -1, -1):
        out = jnp.where(k == i, jnp.float32(values[i]), out)
    return out


def kernel(
    block_ref, pot_ref, idx_ref, val_ref, str_ref, stored_ref,
    out_ref, int_ref,
    field, raw, halo_x, halo_y, beta, pot, sraw, s_hi, s_lo, other, wmat,
    pbuf, r1, g2, q3, csend, crecv,
    in_sem, st_sem, hs_sem, hr_sem, b_sem, p1s, p1r, p2s, p2r, p3s, p3r, cs_sem, cr_sem,
):
    gx = lax.axis_index("gx")
    gyz = lax.axis_index("gyz")
    band = lax.axis_index("band")
    mz = lax.div(gyz, NG_Y)
    my = lax.rem(gyz, NG_Y)
    plane = gx * NG_Y + my
    xl = (lax.rem(gx + NG_X - 1, NG_X), gyz, band)
    xr = (lax.rem(gx + 1, NG_X), gyz, band)
    yl = (gx, lax.rem(gyz + NG_Y * NG_Z - 1, NG_Y * NG_Z), band)
    yr = (gx, lax.rem(gyz + 1, NG_Y * NG_Z), band)
    twin = (gx, gyz, 1 - band)

    def plane_peer(i):
        at = lax.rem(plane + i, PLANE)
        return at, (lax.div(at, NG_Y), mz * NG_Y + lax.rem(at, NG_Y), band)

    def z_peer(i):
        at = lax.rem(mz + i, NG_Z)
        return at, (gx, at * NG_Y + my, band)

    barrier = pltpu.get_barrier_semaphore()

    def greet(device):
        pl.semaphore_signal(barrier, inc=1, device_id=device, device_id_type=MESH)

    for device in (yl, yr, twin):
        greet(device)
    for i in range(1, PLANE):
        greet(plane_peer(i)[1])
    for i in range(1, NG_Z):
        greet(z_peer(i)[1])

    load_block = pltpu.make_async_copy(block_ref, raw, in_sem)
    load_block.start()
    rows = NJ * NXY // DEGREE

    def load_stored(k):
        at = pl.ds(pl.multiple_of(k * rows, rows), rows)
        return pltpu.make_async_copy(stored_ref.at[at], sraw.at[at], st_sem.at[k])

    load_block.wait()
    for k in range(DEGREE):
        load_stored(k).start()

    for xy in range(NXY):
        field[0, xy // CY, xy % CY] = raw[pl.ds(xy, ORB, stride=NXY), :]
    field[1] = jnp.zeros((CX, CY, ORB, CZ), F32)

    pl.semaphore_wait(barrier, 3 + PLANE - 1 + NG_Z - 1)

    def halo_copies(slot):
        def copy(src, dst, n, device):
            return pltpu.make_async_remote_copy(
                src_ref=src, dst_ref=dst, send_sem=hs_sem.at[slot, n], recv_sem=hr_sem.at[slot, n],
                device_id=device, device_id_type=MESH)
        return (
            copy(field.at[slot, 0], halo_x.at[slot, 1], 1, xl),
            copy(field.at[slot, CX - 1], halo_x.at[slot, 0], 0, xr),
            copy(field.at[slot, :, 0], halo_y.at[slot, 1], 3, yl),
            copy(field.at[slot, :, CY - 1], halo_y.at[slot, 0], 2, yr),
        )

    def prepare():
        pot[...] = jnp.broadcast_to(
            (pot_ref[...] + (3.0 - CENTER))[:, None, :], (NXY, ORB, CZ)).reshape(CX, CY, ORB, CZ)
        for p in range(NPROJ):
            index = idx_ref[p:p + 1, :]
            value = val_ref[p:p + 1, :]
            v1 = value.astype(BF16).astype(F32)
            v2 = (value - v1).astype(BF16).astype(F32)
            v3 = value - v1 - v2
            high = lax.shift_right_logical(index, 7)
            low = lax.bitwise_and(index, 127)
            at_xy = lax.broadcasted_iota(jnp.int32, (NXY, 128), 0) == high
            at_z = lax.broadcasted_iota(jnp.int32, (CZ, 128), 0) == low
            left = jnp.concatenate([jnp.where(at_xy, v, 0.0) for v in (v1, v2, v3)], axis=0).astype(BF16)
            right = jnp.where(at_z, 1.0, 0.0).astype(BF16)
            got = lax.dot_general(left, right, (((1,), (1,)), ((), ())), preferred_element_type=F32)
            dense = got[0:NXY] + got[NXY:2 * NXY] + got[2 * NXY:]
            beta[p] = jnp.broadcast_to(dense[:, None, :], (NXY, ORB, CZ)).reshape(CX, CY, ORB, CZ)

    lane = lax.broadcasted_iota(jnp.int32, (CY, ORB, CZ), 2)

    def local(slot, scale, back):
        weights = []
        whole = field[slot]
        for p in range(NPROJ):
            acc = jnp.sum(whole * beta[p], axis=(0, 1))
            weights.append(jnp.sum(acc, axis=1, keepdims=True) * str_ref[p])
        zero = jnp.zeros((1, ORB, CZ), F32)
        for x in range(CX):
            cur = field[slot, x]
            near = jnp.concatenate([zero, cur[:-1]], axis=0) + jnp.concatenate([cur[1:], zero], axis=0)
            near = near + jnp.where(lane == 0, 0.0, pltpu.roll(cur, 1, 2))
            near = near + jnp.where(lane == CZ - 1, 0.0, pltpu.roll(cur, CZ - 1, 2))
            if x > 0:
                near = near + field[slot, x - 1]
            if x < CX - 1:
                near = near + field[slot, x + 1]
            total = pot[x] * cur - 0.5 * near
            for p in range(NPROJ):
                total = total + weights[p][None] * beta[p, x]
            field[1 - slot, x] = scale * total - back * field[1 - slot, x]

    def split_stored(k):
        load_stored(k).wait()
        first = pl.multiple_of(k * (NJ // DEGREE), NJ // DEGREE)
        base = k * rows

        def part(xy, carry):
            got = sraw[pl.ds(base + xy, NJ // DEGREE, stride=NXY), :]
            high = got.astype(BF16)
            cols = pl.ds(pl.multiple_of(xy * CZ, CZ), CZ)
            s_hi[pl.ds(first, NJ // DEGREE), cols] = high
            s_lo[pl.ds(first, NJ // DEGREE), cols] = (got - high.astype(F32)).astype(BF16)
            return carry

        lax.fori_loop(0, NXY, part, 0)

    def step(k, carry):
        slot = lax.rem(k, 2)
        copies = halo_copies(slot)
        for c in copies:
            c.start()

        @pl.when(k == 0)
        def _():
            prepare()

        @pl.when(k > 0)
        def _():
            for c in halo_copies(1 - slot):
                c.wait_send()

        scale = pick(k, SCALES)
        local(slot, scale, pick(k, BACKS))
        split_stored(k)
        for c in copies:
            c.wait_recv()
        factor = -0.5 * scale
        nxt = 1 - slot
        field[nxt, 0] = field[nxt, 0] + factor * halo_x[slot, 0]
        field[nxt, CX - 1] = field[nxt, CX - 1] + factor * halo_x[slot, 1]
        field[nxt, :, 0] = field[nxt, :, 0] + factor * halo_y[slot, 0]
        field[nxt, :, CY - 1] = field[nxt, :, CY - 1] + factor * halo_y[slot, 1]
        return carry

    lax.fori_loop(0, DEGREE, step, 0)
    for c in halo_copies((DEGREE - 1) % 2):
        c.wait_send()

    swap = pltpu.make_async_remote_copy(
        src_ref=field.at[0], dst_ref=other, send_sem=b_sem.at[0], recv_sem=b_sem.at[1],
        device_id=twin, device_id_type=MESH)
    swap.start()
    swap.wait()

    first_core = band == 0
    for xy in range(NXY):
        mine, theirs = field[0, xy // CY, xy % CY], other[xy // CY, xy % CY]
        both = jnp.concatenate(
            [jnp.where(first_core, mine, theirs), jnp.where(first_core, theirs, mine)], axis=0)
        high = both.astype(BF16)
        wmat[0:16, xy * CZ:(xy + 1) * CZ] = high
        wmat[16:32, xy * CZ:(xy + 1) * CZ] = (both - high.astype(F32)).astype(BF16)

    def send1(c):
        return pltpu.make_async_remote_copy(
            src_ref=pbuf.at[c], dst_ref=r1.at[mz], send_sem=p1s.at[c], recv_sem=p1r.at[mz],
            device_id=(gx, c * NG_Y + my, band), device_id_type=MESH)

    nt = (((1,), (1,)), ((), ()))
    for t in range(NJ // 128):
        weights = wmat[...]
        got = lax.dot_general(s_hi[t * 128:(t + 1) * 128, :], weights, nt, preferred_element_type=F32)
        got = got + lax.dot_general(s_lo[t * 128:(t + 1) * 128, :], weights, nt, preferred_element_type=F32)
        flat = got.T
        flat = flat[0:16] + flat[16:32]
        for h in range(2):
            c = 2 * t + h
            pbuf[c] = flat[8 * h:8 * h + 8]

            @pl.when(mz == c)
            def _(c=c):
                r1[c] = pbuf[c]

            @pl.when(mz != c)
            def _(c=c):
                send1(c).start()

    def recv1(i):
        at, device = z_peer(i)
        return pltpu.make_async_remote_copy(
            src_ref=pbuf.at[at], dst_ref=r1.at[at], send_sem=p1s.at[at], recv_sem=p1r.at[at],
            device_id=device, device_id_type=MESH)

    for i in range(1, NG_Z):
        recv1(i).wait_recv()
    g2[plane] = jnp.sum(r1[...], axis=0)

    def send2(i):
        return pltpu.make_async_remote_copy(
            src_ref=g2.at[plane], dst_ref=g2.at[plane], send_sem=p2s.at[i], recv_sem=p2r.at[plane],
            device_id=plane_peer(i)[1], device_id_type=MESH)

    def recv2(i):
        at, device = plane_peer(i)
        return pltpu.make_async_remote_copy(
            src_ref=g2.at[plane], dst_ref=g2.at[at], send_sem=p2s.at[i], recv_sem=p2r.at[at],
            device_id=device, device_id_type=MESH)

    for i in range(1, PLANE):
        send2(i).start()
    for i in range(1, NG_Z):
        recv1(i).wait_send()
    for i in range(1, PLANE):
        recv2(i).wait_recv()
    q3[mz] = jnp.sum(g2[...], axis=0)

    def send3(i):
        return pltpu.make_async_remote_copy(
            src_ref=q3.at[mz], dst_ref=q3.at[mz], send_sem=p3s.at[i], recv_sem=p3r.at[mz],
            device_id=z_peer(i)[1], device_id_type=MESH)

    def recv3(i):
        at, device = z_peer(i)
        return pltpu.make_async_remote_copy(
            src_ref=q3.at[mz], dst_ref=q3.at[at], send_sem=p3s.at[i], recv_sem=p3r.at[at],
            device_id=device, device_id_type=MESH)

    for i in range(1, NG_Z):
        send3(i).start()
    for i in range(1, PLANE):
        send2(i).wait_send()
    for i in range(1, NG_Z):
        recv3(i).wait_recv()

    whole = jnp.concatenate(
        [jnp.concatenate([q3[2 * t], q3[2 * t + 1]], axis=0) for t in range(NJ // 128)], axis=1)
    int_ref[...] = whole
    high = whole.astype(BF16)
    low = (whole - high.astype(F32)).astype(BF16)
    left = jnp.concatenate([high, low], axis=0)
    nn = (((1,), (0,)), ((), ()))

    def give(x):
        return pltpu.make_async_remote_copy(
            src_ref=csend.at[x], dst_ref=crecv.at[x], send_sem=cs_sem.at[x], recv_sem=cr_sem.at[x],
            device_id=twin, device_id_type=MESH)

    for x in range(CX):
        cols = slice(x * CY * CZ, (x + 1) * CY * CZ)
        got = lax.dot_general(left, s_hi[:, cols], nn, preferred_element_type=F32)
        more = lax.dot_general(high, s_lo[:, cols], nn, preferred_element_type=F32)
        got = got[0:16] + got[16:32] + more
        keep = jnp.where(first_core, got[0:8], got[8:16])
        send = jnp.where(first_core, got[8:16], got[0:8])
        for y in range(CY):
            csend[x, y] = send[:, y * CZ:(y + 1) * CZ]
            field[1, x, y] = field[0, x, y] - keep[:, y * CZ:(y + 1) * CZ]
        give(x).start()
    for i in range(1, NG_Z):
        send3(i).wait_send()
    for x in range(CX):
        give(x).wait_recv()
        for y in range(CY):
            out_ref[pl.ds(x * CY + y, ORB, stride=NXY), :] = field[1, x, y] - crecv[x, y]
    for x in range(CX):
        give(x).wait_send()


def on_device(block, potential, proj_index, proj_value, proj_strength, stored):
    vmem = pl.BlockSpec(memory_space=pltpu.VMEM)
    dma = pltpu.SemaphoreType.DMA
    projected, intersection = pl.pallas_call(
        kernel,
        out_shape=(
            jax.ShapeDtypeStruct((ORB * NXY, CZ), F32),
            jax.ShapeDtypeStruct((2 * ORB, NJ), F32),
        ),
        in_specs=[
            pl.BlockSpec(memory_space=pl.ANY), vmem, vmem, vmem,
            pl.BlockSpec(memory_space=pltpu.SMEM), pl.BlockSpec(memory_space=pl.ANY)],
        out_specs=(vmem, vmem),
        scratch_shapes=[
            pltpu.VMEM((2, CX, CY, ORB, CZ), F32),
            pltpu.VMEM((ORB * NXY, CZ), F32),
            pltpu.VMEM((2, 2, CY, ORB, CZ), F32),
            pltpu.VMEM((2, 2, CX, ORB, CZ), F32),
            pltpu.VMEM((NPROJ, CX, CY, ORB, CZ), F32),
            pltpu.VMEM((CX, CY, ORB, CZ), F32),
            pltpu.VMEM((NJ * NXY, CZ), F32),
            pltpu.VMEM((NJ, CELLS), BF16),
            pltpu.VMEM((NJ, CELLS), BF16),
            pltpu.VMEM((CX, CY, ORB, CZ), F32),
            pltpu.VMEM((4 * ORB, CELLS), BF16),
            pltpu.VMEM((NG_Z, ORB, CZ), F32),
            pltpu.VMEM((NG_Z, ORB, CZ), F32),
            pltpu.VMEM((PLANE, ORB, CZ), F32),
            pltpu.VMEM((NG_Z, ORB, CZ), F32),
            pltpu.VMEM((CX, CY, ORB, CZ), F32),
            pltpu.VMEM((CX, CY, ORB, CZ), F32),
            dma, dma((DEGREE,)), dma((2, 4)), dma((2, 4)), dma((2,)),
            dma((NG_Z,)), dma((NG_Z,)), dma((PLANE,)), dma((PLANE,)), dma((NG_Z,)), dma((NG_Z,)),
            dma((CX,)), dma((CX,)),
        ],
        compiler_params=pltpu.CompilerParams(
            collective_id=0, has_side_effects=True, vmem_limit_bytes=40 * 1024 * 1024),
        name="filter_project",
    )(
        block.reshape(ORB * NXY, CZ), potential.reshape(NXY, CZ), proj_index, proj_value,
        proj_strength, stored.reshape(NJ * NXY, CZ))
    return projected.reshape(block.shape), intersection.T


def solution(mesh):
    in_specs = (
        P("band", "gx", "gyz", None),
        P("gx", "gyz", None),
        P(("gx", "gyz"), None),
        P(("gx", "gyz"), None),
        P(("gx", "gyz")),
        P("band", "gx", "gyz", None),
    )
    out_specs = (P("band", "gx", "gyz", None), P("band", None))
    return jax.shard_map(
        on_device, mesh=mesh, in_specs=in_specs, out_specs=out_specs, check_vma=False
    )
```

time: 921 us -> 78.6 us (0.09)
  blocking collectives: 588 us -> 0 us
  waiting for transfers between devices: 134 us -> 0 us
  Pallas kernels: 0 us -> 69.4 us
  other arithmetic: 59 us -> 0 us
  starting transfers between devices: 57.1 us -> 0 us
  matrix products: 26.4 us -> 0 us
  local copies, waits for them, and re-layouts: 34.6 us -> 8.29 us
  between operations: 15.1 us -> 0.65 us
    psum x1 -> x0, blocking collectives: 571 us -> none  [on_device(): intersection = lax.psum(partial_intersection, ('gx', 'gyz'))]
    reduce_scatter x1 -> x0, waiting for transfers between devices: 115 us -> none  [on_device(): lax.psum_scatter(jnp.dot(intersection.T, flat_stored, precision=lax.Preci...]
    pallas_call x0 -> x1, Pallas kernels: none -> 69.4 us  [on_device(): pl.pallas_call(kernel, out_shape=(jax.ShapeDtypeStruct((ORB * NXY, CZ), F...]
    ppermute x32 -> x0, starting transfers between devices: 57.1 us -> none  [the longest x16 44.6 us: extended(): lax.ppermute(head, axis, [((i + 1) % count, i) for i in range(count)])]
    scatter-add x8 -> x0, other arithmetic: 53 us -> none  [nonlocal_term(): return jnp.zeros_like(flat_block).at[:, cell_index].add(spread)]
    dot_general x2 -> x0, matrix products: 26.4 us -> none  [the longest x1 13.7 us: on_device(): jnp.dot(flat_stored, flat_filtered.T, precision=lax.Precision.HIGHEST)]
    gather x8 -> x0, local copies, waits for them, and re-layouts: 22.5 us -> none  [nonlocal_term(): picked = flat_block[:, cell_index]]
    ppermute x32 -> x0, waiting for transfers between devices: 18.9 us -> none  [the longest x16 10.3 us: extended(): lax.ppermute(tail, axis, [(i, (i + 1) % count) for i in range(count)])]
  transfers between devices with their start and end apart: 33 -> 0, of which waited for: 15 -> 0; matrix products, arithmetic and copies ran while one was open for 7% -> 0% of each run, Pallas kernels for 0% -> 0%
where the time goes in v1:
time: 78.6 us; the launch traced here: 78.4 us
  Pallas kernels  69.4 us (88%)
  local copies, waits for them, and re-layouts  8.29 us (11%)
    pallas_call x1, Pallas kernels, on_device(): pl.pallas_call(kernel, out_shape=(jax.ShapeDtypeStruct((ORB * NXY, CZ), F...  69.4 us
    unnamed x14, local copies, waits for them, and re-layouts  8.29 us

profile of v1, /device:TPU:1, one launch (start us, length us, event | category | flops | bytes accessed | tf_op | source)
XLA Modules:
  0.0 78.4 jit_solution(8581831060698569854)
XLA Ops:
  0.6 0.0 copy-start
  0.6 3.4 %copy-done = f32[512,4,8,128]{3,2,1,0:T(8,128)S(1)} copy-done((f32[512,4,8,128]{3,2,1,0:T(8,128)S(1)}, f32[512,4,8,128]{3,2,1,0:T(8,128)}, u32[]{:S(2)}) %copy-start) | copy-done | bytes 8388632
  4.0 0.0 copy-start.1
  4.0 0.9 %copy-done.1 = f32[8,4,8,128]{3,2,1,0:T(8,128)S(1)} copy-done((f32[8,4,8,128]{3,2,1,0:T(8,128)S(1)}, f32[8,4,8,128]{3,2,1,0:T(8,128)}, u32[]{:S(2)}) %copy-start.1) | copy-done | bytes 131096
  4.9 0.0 copy-start.2
  4.9 0.7 copy-done.2
  5.6 0.0 copy-start.3
  5.6 0.7 copy-done.3
  6.3 0.0 copy-start.4
  6.3 0.7 copy-done.4
  7.0 0.0 copy-start.5
  7.0 0.7 copy-done.5
  7.7 69.4 %filter_project.1 = (f32[256,128]{1,0:T(8,128)S(1)}, f32[16,512]{1,0:T(8,128)S(1)}) custom-call(f32[256,128]{1,0:T(8,128)S(1)} %bitcast.6, f32[32,128]{1,0:T(8,128)S(1)} %bitcast.9, s32[8,128]{1,0:T(8,128)S(1)} %copy-done.3, f32[8,128]{1,0:T(8,128)S(1)} %copy-done.4, f32[8]{0:T(128)S(1)} %copy-done.5, f32[16384,128]{1,0:T(8,128)S(1)} %bitcast.5), custom_call_target="tpu_custom_call" | custom-call | tf_op jit(solution)/shard_map/filter_project/pallas_call | solution.py:334
  77.1 0.7 copy.10
  77.8 0.6 copy.11
Async XLA Ops:
  0.6 3.4 %copy-start = (f32[512,4,8,128]{3,2,1,0:T(8,128)S(1)}, f32[512,4,8,128]{3,2,1,0:T(8,128)}, u32[]{:S(2)}) copy-start(f32[512,4,8,128]{3,2,1,0:T(8,128)} %param.11) | copy-start | bytes 25165828
  4.0 0.9 %copy-start.1 = (f32[8,4,8,128]{3,2,1,0:T(8,128)S(1)}, f32[8,4,8,128]{3,2,1,0:T(8,128)}, u32[]{:S(2)}) copy-start(f32[8,4,8,128]{3,2,1,0:T(8,128)} %param.6) | copy-start | bytes 393220
  4.9 0.7 copy-start.2
  5.6 0.7 copy-start.3
  6.3 0.7 copy-start.4
  7.0 0.7 copy-start.5

commit v2 on v1

--- a/solution.py
+++ b/solution.py
@@ -8,6 +8,7 @@
 from jax.sharding import PartitionSpec as P
 
 DEGREE = 8
+ROUNDS = DEGREE // 2
 LOW_EDGE = 0.0
 CUT_EDGE = 1.0
 TOP_EDGE = 10.0
@@ -29,18 +30,20 @@
 
 
 def recurrence():
-    first = HALF / (LOW_EDGE - CENTER)
-    scales, backs = [first / HALF], [0.0]
-    now = first
-    for _ in range(DEGREE - 1):
-        after = 1.0 / (2.0 / first - now)
-        scales.append(2.0 * after / HALF)
-        backs.append(now * after)
-        now = after
-    return scales, backs
-
-
-SCALES, BACKS = recurrence()
+    x = (LOW_EDGE - CENTER) / HALF
+    t = [1.0, x]
+    while len(t) <= DEGREE:
+        t.append(2.0 * x * t[-1] - t[-2])
+    ups, stays, backs = [2.0 / t[2]], [-1.0 / t[2]], [0.0]
+    for m in range(1, ROUNDS):
+        after = t[2 * m + 2]
+        ups.append(4.0 * t[2 * m] / after)
+        stays.append(-2.0 * t[2 * m] / after)
+        backs.append(t[2 * m - 2] / after)
+    return ups, stays, backs
+
+
+UPS, STAYS, BACKS = recurrence()
 
 
 def pick(k, values):
@@ -53,9 +56,9 @@
 def kernel(
     block_ref, pot_ref, idx_ref, val_ref, str_ref, stored_ref,
     out_ref, int_ref,
-    field, raw, halo_x, halo_y, beta, pot, sraw, s_hi, s_lo, other, wmat,
+    field, inner, raw, beta, dense, edge, side_x, side_y, beta_x, beta_y, coef, coef_in, sraw, s_hi, s_lo, other, wmat,
     pbuf, r1, g2, q3, csend, crecv,
-    in_sem, st_sem, hs_sem, hr_sem, b_sem, p1s, p1r, p2s, p2r, p3s, p3r, cs_sem, cr_sem,
+    in_sem, st_sem, hs_sem, hr_sem, fs_sem, fr_sem, b_sem, p1s, p1r, p2s, p2r, p3s, p3r, cs_sem, cr_sem,
 ):
     gx = lax.axis_index("gx")
     gyz = lax.axis_index("gyz")
@@ -63,10 +66,10 @@
     mz = lax.div(gyz, NG_Y)
     my = lax.rem(gyz, NG_Y)
     plane = gx * NG_Y + my
-    xl = (lax.rem(gx + NG_X - 1, NG_X), gyz, band)
-    xr = (lax.rem(gx + 1, NG_X), gyz, band)
-    yl = (gx, lax.rem(gyz + NG_Y * NG_Z - 1, NG_Y * NG_Z), band)
-    yr = (gx, lax.rem(gyz + 1, NG_Y * NG_Z), band)
+    left, right = lax.rem(gx + NG_X - 1, NG_X), lax.rem(gx + 1, NG_X)
+    down, up = lax.rem(gyz + NG_Y * NG_Z - 1, NG_Y * NG_Z), lax.rem(gyz + 1, NG_Y * NG_Z)
+    xl, xr, yl, yr = (left, gyz, band), (right, gyz, band), (gx, down, band), (gx, up, band)
+    diagonal = [(x, y, band) for x in (left, right) for y in (down, up)]
     twin = (gx, gyz, 1 - band)
 
     def plane_peer(i):
@@ -82,7 +85,7 @@
     def greet(device):
         pl.semaphore_signal(barrier, inc=1, device_id=device, device_id_type=MESH)
 
-    for device in (yl, yr, twin):
+    for device in [yl, yr, twin] + diagonal:
         greet(device)
     for i in range(1, PLANE):
         greet(plane_peer(i)[1])
@@ -97,69 +100,152 @@
         at = pl.ds(pl.multiple_of(k * rows, rows), rows)
         return pltpu.make_async_copy(stored_ref.at[at], sraw.at[at], st_sem.at[k])
 
-    load_block.wait()
-    for k in range(DEGREE):
-        load_stored(k).start()
-
-    for xy in range(NXY):
-        field[0, xy // CY, xy % CY] = raw[pl.ds(xy, ORB, stride=NXY), :]
-    field[1] = jnp.zeros((CX, CY, ORB, CZ), F32)
-
-    pl.semaphore_wait(barrier, 3 + PLANE - 1 + NG_Z - 1)
-
-    def halo_copies(slot):
-        def copy(src, dst, n, device):
-            return pltpu.make_async_remote_copy(
-                src_ref=src, dst_ref=dst, send_sem=hs_sem.at[slot, n], recv_sem=hr_sem.at[slot, n],
-                device_id=device, device_id_type=MESH)
-        return (
-            copy(field.at[slot, 0], halo_x.at[slot, 1], 1, xl),
-            copy(field.at[slot, CX - 1], halo_x.at[slot, 0], 0, xr),
-            copy(field.at[slot, :, 0], halo_y.at[slot, 1], 3, yl),
-            copy(field.at[slot, :, CY - 1], halo_y.at[slot, 0], 2, yr),
-        )
-
     def prepare():
-        pot[...] = jnp.broadcast_to(
-            (pot_ref[...] + (3.0 - CENTER))[:, None, :], (NXY, ORB, CZ)).reshape(CX, CY, ORB, CZ)
+        low_edge = lax.broadcasted_iota(jnp.int32, (NXY, 128), 0)
+        at_row = lax.broadcasted_iota(jnp.int32, (CZ, 128), 0)
         for p in range(NPROJ):
             index = idx_ref[p:p + 1, :]
             value = val_ref[p:p + 1, :]
             v1 = value.astype(BF16).astype(F32)
             v2 = (value - v1).astype(BF16).astype(F32)
             v3 = value - v1 - v2
-            high = lax.shift_right_logical(index, 7)
-            low = lax.bitwise_and(index, 127)
-            at_xy = lax.broadcasted_iota(jnp.int32, (NXY, 128), 0) == high
-            at_z = lax.broadcasted_iota(jnp.int32, (CZ, 128), 0) == low
-            left = jnp.concatenate([jnp.where(at_xy, v, 0.0) for v in (v1, v2, v3)], axis=0).astype(BF16)
-            right = jnp.where(at_z, 1.0, 0.0).astype(BF16)
-            got = lax.dot_general(left, right, (((1,), (1,)), ((), ())), preferred_element_type=F32)
-            dense = got[0:NXY] + got[NXY:2 * NXY] + got[2 * NXY:]
-            beta[p] = jnp.broadcast_to(dense[:, None, :], (NXY, ORB, CZ)).reshape(CX, CY, ORB, CZ)
-
-    lane = lax.broadcasted_iota(jnp.int32, (CY, ORB, CZ), 2)
-
-    def local(slot, scale, back):
-        weights = []
-        whole = field[slot]
+            at_xy = low_edge == lax.shift_right_logical(index, 7)
+            at_z = at_row == lax.bitwise_and(index, 127)
+            picks = jnp.concatenate([jnp.where(at_xy, v, 0.0) for v in (v1, v2, v3)], axis=0).astype(BF16)
+            places = jnp.where(at_z, 1.0, 0.0).astype(BF16)
+            got = lax.dot_general(picks, places, (((1,), (1,)), ((), ())), preferred_element_type=F32)
+            dense[p] = got[0:NXY] + got[NXY:2 * NXY] + got[2 * NXY:]
+        dense[NPROJ] = (pot_ref[...] + (3.0 - CENTER)) * (1.0 / HALF)
+        for p in range(NPROJ + 1):
+            beta[p] = jnp.broadcast_to(dense[p][:, None, :], (NXY, ORB, CZ)).reshape(CX, CY, ORB, CZ)
+            edge[p, 0:4] = dense[p, pl.ds(0, CX, stride=CY), :]
+            edge[p, 4:8] = dense[p, pl.ds(CY - 1, CX, stride=CY), :]
+
+    def side_copies():
+        def copy(src, dst, n, device):
+            return pltpu.make_async_remote_copy(
+                src_ref=src, dst_ref=dst, send_sem=fs_sem.at[n], recv_sem=fr_sem.at[n],
+                device_id=device, device_id_type=MESH)
+        return (
+            copy(dense.at[:, 0:CY], side_x.at[1], 1, xl),
+            copy(dense.at[:, NXY - CY:NXY], side_x.at[0], 0, xr),
+            copy(edge, side_y.at[1], 3, yl),
+            copy(edge, side_y.at[0], 2, yr),
+        )
+
+    def spread_sides():
+        for p in range(NPROJ + 1):
+            for side in range(2):
+                beta_x[side, p] = jnp.broadcast_to(side_x[side, p][:, None, :], (CY, ORB, CZ))
+                rows_y = side_y[side, p, 4:8] if side == 0 else side_y[side, p, 0:4]
+                beta_y[side, p] = jnp.broadcast_to(rows_y[:, None, :], (CX, ORB, CZ))
+
+    load_block.wait()
+    for k in range(DEGREE):
+        load_stored(k).start()
+
+    for xy in range(NXY):
+        field[0, 2 + xy // CY, 2 + xy % CY] = raw[pl.ds(xy, ORB, stride=NXY), :]
+    field[1, 2:6, 2:10] = jnp.zeros((CX, CY, ORB, CZ), F32)
+    prepare()
+
+    pl.semaphore_wait(barrier, 7 + PLANE - 1 + NG_Z - 1)
+
+    def halo_copies(slot):
+        def copy(src, dst, n, device):
+            return pltpu.make_async_remote_copy(
+                src_ref=field.at[(slot,) + src], dst_ref=field.at[(slot,) + dst],
+                send_sem=hs_sem.at[slot, n], recv_sem=hr_sem.at[slot, n],
+                device_id=device, device_id_type=MESH)
+        own_x, own_y = slice(2, 6), slice(2, 10)
+        return (
+            copy((2, 2), (6, 10), 4, diagonal[0]),
+            copy((2, 9), (6, 1), 5, diagonal[1]),
+            copy((5, 2), (1, 10), 6, diagonal[2]),
+            copy((5, 9), (1, 1), 7, diagonal[3]),
+            copy((own_x, slice(2, 4)), (own_x, slice(10, 12)), 3, yl),
+            copy((own_x, slice(8, 10)), (own_x, slice(0, 2)), 2, yr),
+            copy((slice(2, 4), own_y), (slice(6, 8), own_y), 1, xl),
+            copy((slice(4, 6), own_y), (slice(0, 2), own_y), 0, xr),
+        )
+
+    def coef_copies(slot):
+        def copy(side, n, device):
+            return pltpu.make_async_remote_copy(
+                src_ref=coef.at[slot], dst_ref=coef_in.at[slot, side],
+                send_sem=hs_sem.at[slot, 8 + n], recv_sem=hr_sem.at[slot, 8 + n],
+                device_id=device, device_id_type=MESH)
+        return copy(3, 3, yl), copy(2, 2, yr), copy(1, 1, xl), copy(0, 0, xr)
+
+    lanes = lax.broadcasted_iota(jnp.int32, (1, ORB, CZ), 2)
+    lane = lax.broadcasted_iota(jnp.int32, (ORB, CZ), 1)
+    side_scale = 0.5 / HALF
+
+    def along_z(cur):
+        return (jnp.where(lanes == 0, 0.0, pltpu.roll(cur, 1, 2))
+                + jnp.where(lanes == CZ - 1, 0.0, pltpu.roll(cur, CZ - 1, 2)))
+
+    def coefficients(whole):
+        out = []
         for p in range(NPROJ):
             acc = jnp.sum(whole * beta[p], axis=(0, 1))
-            weights.append(jnp.sum(acc, axis=1, keepdims=True) * str_ref[p])
+            out.append(jnp.sum(acc, axis=1, keepdims=True) * (str_ref[p] * (1.0 / HALF)))
+        return out
+
+    def spread(weights, tiles):
+        total = weights[0][None] * tiles(0)
+        for p in range(1, NPROJ):
+            total = total + weights[p][None] * tiles(p)
+        return total
+
+    def first_inside(slot, weights):
         zero = jnp.zeros((1, ORB, CZ), F32)
         for x in range(CX):
-            cur = field[slot, x]
+            cur = field[slot, 2 + x, 2:10]
             near = jnp.concatenate([zero, cur[:-1]], axis=0) + jnp.concatenate([cur[1:], zero], axis=0)
-            near = near + jnp.where(lane == 0, 0.0, pltpu.roll(cur, 1, 2))
-            near = near + jnp.where(lane == CZ - 1, 0.0, pltpu.roll(cur, CZ - 1, 2))
+            near = near + along_z(cur)
             if x > 0:
-                near = near + field[slot, x - 1]
+                near = near + field[slot, 1 + x, 2:10]
             if x < CX - 1:
-                near = near + field[slot, x + 1]
-            total = pot[x] * cur - 0.5 * near
-            for p in range(NPROJ):
-                total = total + weights[p][None] * beta[p, x]
-            field[1 - slot, x] = scale * total - back * field[1 - slot, x]
+                near = near + field[slot, 3 + x, 2:10]
+            inner[1 + x, 1:9] = (
+                beta[NPROJ, x] * cur - side_scale * near + spread(weights, lambda p: beta[p, x]))
+
+    def first_outside(slot):
+        inner[1, 1:9] = inner[1, 1:9] - side_scale * field[slot, 1, 2:10]
+        inner[4, 1:9] = inner[4, 1:9] - side_scale * field[slot, 6, 2:10]
+        inner[1:5, 1] = inner[1:5, 1] - side_scale * field[slot, 2:6, 1]
+        inner[1:5, 8] = inner[1:5, 8] - side_scale * field[slot, 2:6, 10]
+        for side in range(2):
+            at = 1 if side == 0 else 6
+            got = coef_in[slot, side]
+            weights = [got[:, p:p + 1] for p in range(NPROJ)]
+            cur = field[slot, at, 2:10]
+            near = field[slot, at - 1, 2:10] + field[slot, at + 1, 2:10]
+            near = near + field[slot, at, 1:9] + field[slot, at, 3:11] + along_z(cur)
+            inner[at - 1, 1:9] = (
+                beta_x[side, NPROJ] * cur - side_scale * near
+                + spread(weights, lambda p: beta_x[side, p]))
+        for side in range(2):
+            at = 1 if side == 0 else 10
+            got = coef_in[slot, 2 + side]
+            weights = [got[:, p:p + 1] for p in range(NPROJ)]
+            cur = field[slot, 2:6, at]
+            near = field[slot, 2:6, at - 1] + field[slot, 2:6, at + 1]
+            near = near + field[slot, 1:5, at] + field[slot, 3:7, at] + along_z(cur)
+            inner[1:5, at - 1] = (
+                beta_y[side, NPROJ] * cur - side_scale * near
+                + spread(weights, lambda p: beta_y[side, p]))
+
+    def second(slot, ups, stays, backs):
+        weights = coefficients(inner[1:5, 1:9])
+        for x in range(CX):
+            cur = inner[1 + x, 1:9]
+            near = inner[x, 1:9] + inner[2 + x, 1:9] + inner[1 + x, 0:8] + inner[1 + x, 2:10]
+            near = near + along_z(cur)
+            twice = beta[NPROJ, x] * cur - side_scale * near + spread(weights, lambda p: beta[p, x])
+            field[1 - slot, 2 + x, 2:10] = (
+                ups * twice + stays * field[slot, 2 + x, 2:10] - backs * field[1 - slot, 2 + x, 2:10])
 
     def split_stored(k):
         load_stored(k).wait()
@@ -184,39 +270,51 @@
 
         @pl.when(k == 0)
         def _():
-            prepare()
+            for c in side_copies():
+                c.start()
+
+        weights = coefficients(field[slot, 2:6, 2:10])
+        packed = jnp.zeros((ORB, CZ), F32)
+        for p in range(NPROJ):
+            packed = jnp.where(lane == p, weights[p], packed)
+        coef[slot] = packed
+        more = coef_copies(slot)
+        for c in more:
+            c.start()
+        first_inside(slot, weights)
+        split_stored(2 * k)
+        split_stored(2 * k + 1)
 
         @pl.when(k > 0)
         def _():
-            for c in halo_copies(1 - slot):
+            for c in halo_copies(1 - slot) + coef_copies(1 - slot):
                 c.wait_send()
 
-        scale = pick(k, SCALES)
-        local(slot, scale, pick(k, BACKS))
-        split_stored(k)
-        for c in copies:
+        @pl.when(k == 0)
+        def _():
+            for c in side_copies():
+                c.wait()
+            spread_sides()
+
+        for c in copies + more:
             c.wait_recv()
-        factor = -0.5 * scale
-        nxt = 1 - slot
-        field[nxt, 0] = field[nxt, 0] + factor * halo_x[slot, 0]
-        field[nxt, CX - 1] = field[nxt, CX - 1] + factor * halo_x[slot, 1]
-        field[nxt, :, 0] = field[nxt, :, 0] + factor * halo_y[slot, 0]
-        field[nxt, :, CY - 1] = field[nxt, :, CY - 1] + factor * halo_y[slot, 1]
+        first_outside(slot)
+        second(slot, pick(k, UPS), pick(k, STAYS), pick(k, BACKS))
         return carry
 
-    lax.fori_loop(0, DEGREE, step, 0)
-    for c in halo_copies((DEGREE - 1) % 2):
+    lax.fori_loop(0, ROUNDS, step, 0)
+    for c in halo_copies((ROUNDS - 1) % 2) + coef_copies((ROUNDS - 1) % 2):
         c.wait_send()
 
     swap = pltpu.make_async_remote_copy(
-        src_ref=field.at[0], dst_ref=other, send_sem=b_sem.at[0], recv_sem=b_sem.at[1],
+        src_ref=field.at[0, 2:6, 2:10], dst_ref=other, send_sem=b_sem.at[0], recv_sem=b_sem.at[1],
         device_id=twin, device_id_type=MESH)
     swap.start()
     swap.wait()
 
     first_core = band == 0
     for xy in range(NXY):
-        mine, theirs = field[0, xy // CY, xy % CY], other[xy // CY, xy % CY]
+        mine, theirs = field[0, 2 + xy // CY, 2 + xy % CY], other[xy // CY, xy % CY]
         both = jnp.concatenate(
             [jnp.where(first_core, mine, theirs), jnp.where(first_core, theirs, mine)], axis=0)
         high = both.astype(BF16)
@@ -316,14 +414,14 @@
         send = jnp.where(first_core, got[8:16], got[0:8])
         for y in range(CY):
             csend[x, y] = send[:, y * CZ:(y + 1) * CZ]
-            field[1, x, y] = field[0, x, y] - keep[:, y * CZ:(y + 1) * CZ]
+            field[1, 2 + x, 2 + y] = field[0, 2 + x, 2 + y] - keep[:, y * CZ:(y + 1) * CZ]
         give(x).start()
     for i in range(1, NG_Z):
         send3(i).wait_send()
     for x in range(CX):
         give(x).wait_recv()
         for y in range(CY):
-            out_ref[pl.ds(x * CY + y, ORB, stride=NXY), :] = field[1, x, y] - crecv[x, y]
+            out_ref[pl.ds(x * CY + y, ORB, stride=NXY), :] = field[1, 2 + x, 2 + y] - crecv[x, y]
     for x in range(CX):
         give(x).wait_send()
 
@@ -342,12 +440,18 @@
             pl.BlockSpec(memory_space=pltpu.SMEM), pl.BlockSpec(memory_space=pl.ANY)],
         out_specs=(vmem, vmem),
         scratch_shapes=[
-            pltpu.VMEM((2, CX, CY, ORB, CZ), F32),
+            pltpu.VMEM((2, CX + 4, CY + 4, ORB, CZ), F32),
+            pltpu.VMEM((CX + 2, CY + 2, ORB, CZ), F32),
             pltpu.VMEM((ORB * NXY, CZ), F32),
-            pltpu.VMEM((2, 2, CY, ORB, CZ), F32),
-            pltpu.VMEM((2, 2, CX, ORB, CZ), F32),
-            pltpu.VMEM((NPROJ, CX, CY, ORB, CZ), F32),
-            pltpu.VMEM((CX, CY, ORB, CZ), F32),
+            pltpu.VMEM((NPROJ + 1, CX, CY, ORB, CZ), F32),
+            pltpu.VMEM((NPROJ + 1, NXY, CZ), F32),
+            pltpu.VMEM((NPROJ + 1, 2 * CX, CZ), F32),
+            pltpu.VMEM((2, NPROJ + 1, CY, CZ), F32),
+            pltpu.VMEM((2, NPROJ + 1, 2 * CX, CZ), F32),
+            pltpu.VMEM((2, NPROJ + 1, CY, ORB, CZ), F32),
+            pltpu.VMEM((2, NPROJ + 1, CX, ORB, CZ), F32),
+            pltpu.VMEM((2, ORB, CZ), F32),
+            pltpu.VMEM((2, 4, ORB, CZ), F32),
             pltpu.VMEM((NJ * NXY, CZ), F32),
             pltpu.VMEM((NJ, CELLS), BF16),
             pltpu.VMEM((NJ, CELLS), BF16),
@@ -359,12 +463,12 @@
             pltpu.VMEM((NG_Z, ORB, CZ), F32),
             pltpu.VMEM((CX, CY, ORB, CZ), F32),
             pltpu.VMEM((CX, CY, ORB, CZ), F32),
-            dma, dma((DEGREE,)), dma((2, 4)), dma((2, 4)), dma((2,)),
+            dma, dma((DEGREE,)), dma((2, 12)), dma((2, 12)), dma((4,)), dma((4,)), dma((2,)),
             dma((NG_Z,)), dma((NG_Z,)), dma((PLANE,)), dma((PLANE,)), dma((NG_Z,)), dma((NG_Z,)),
             dma((CX,)), dma((CX,)),
         ],
         compiler_params=pltpu.CompilerParams(
-            collective_id=0, has_side_effects=True, vmem_limit_bytes=40 * 1024 * 1024),
+            collective_id=0, has_side_effects=True, vmem_limit_bytes=60 * 1024 * 1024),
         name="filter_project",
     )(
         block.reshape(ORB * NXY, CZ), potential.reshape(NXY, CZ), proj_index, proj_value,

time: 78.6 us -> 61.8 us (0.79)
  Pallas kernels: 69.4 us -> 58 us
  local copies, waits for them, and re-layouts: 8.29 us -> 2.94 us
    pallas_call x1, Pallas kernels: 69.4 us -> 58 us  [on_device(): pl.pallas_call(kernel, out_shape=(jax.ShapeDtypeStruct((ORB * NXY, CZ), F...]
    unnamed x14 -> x2, local copies, waits for them, and re-layouts: 8.29 us -> 2.94 us
where the time goes in v2:
time: 61.8 us; the launch traced here: 61.5 us
  Pallas kernels  58 us (94%)
  local copies, waits for them, and re-layouts  2.94 us (5%)
  between operations  0.64 us (1%)
    pallas_call x1, Pallas kernels, on_device(): pl.pallas_call(kernel, out_shape=(jax.ShapeDtypeStruct((ORB * NXY, CZ), F...  58 us
    unnamed x2, local copies, waits for them, and re-layouts  2.94 us

profile of v2, /device:TPU:1, one launch (start us, length us, event | category | flops | bytes accessed | tf_op | source)
XLA Modules:
  0.0 61.5 jit_solution(12118197674806165937)
XLA Ops:
  0.6 58.0 %filter_project.1 = (f32[256,128]{1,0:T(8,128)}, f32[16,512]{1,0:T(8,128)}) custom-call(f32[256,128]{1,0:T(8,128)} %bitcast.6, f32[32,128]{1,0:T(8,128)} %bitcast.9, s32[8,128]{1,0:T(8,128)} %idx_ref.1, f32[8,128]{1,0:T(8,128)} %val_ref.1, f32[8]{0:T(128)} %str_ref.1, f32[16384,128]{1,0:T(8,128)} %bitcast.5), custom_call_target="tpu_custom_call" | custom-call | tf_op jit(solution)/shard_map/filter_project/pallas_call | solution.py:432
  58.6 1.6 %copy.10 = f32[8,4,8,128]{3,2,1,0:T(8,128)} copy(f32[8,4,8,128]{3,2,1,0:T(8,128)} %bitcast.7) | data formatting | bytes 262144
  60.2 1.4 %copy.11 = f32[512,16]{0,1:T(8,128)} copy(f32[512,16]{0,1:T(8,128)} %bitcast.8) | data formatting | bytes 65536

commit v3 on v2

--- a/solution.py
+++ b/solution.py
@@ -54,11 +54,11 @@
 
 
 def kernel(
-    block_ref, pot_ref, idx_ref, val_ref, str_ref, stored_ref,
+    block_ref, pot_in, idx_in, val_in, str_ref, stored_ref,
     out_ref, int_ref,
-    field, inner, raw, beta, dense, edge, side_x, side_y, beta_x, beta_y, coef, coef_in, sraw, s_hi, s_lo, other, wmat,
+    field, inner, raw, pot_ref, idx_ref, val_ref, beta, dense, edge, side_x, side_y, beta_x, beta_y, coef, coef_in, sraw, s_hi, s_lo, other, wmat, total,
     pbuf, r1, g2, q3, csend, crecv,
-    in_sem, st_sem, hs_sem, hr_sem, fs_sem, fr_sem, b_sem, p1s, p1r, p2s, p2r, p3s, p3r, cs_sem, cr_sem,
+    in_sem, st_sem, hs_sem, hr_sem, fs_sem, fr_sem, bs_sem, br_sem, p1s, p1r, p2s, p2r, p3s, p3r, cs_sem, cr_sem,
 ):
     gx = lax.axis_index("gx")
     gyz = lax.axis_index("gyz")
@@ -92,8 +92,12 @@
     for i in range(1, NG_Z):
         greet(z_peer(i)[1])
 
-    load_block = pltpu.make_async_copy(block_ref, raw, in_sem)
-    load_block.start()
+    loads = [
+        pltpu.make_async_copy(src, dst, in_sem.at[n])
+        for n, (src, dst) in enumerate(
+            ((idx_in, idx_ref), (val_in, val_ref), (pot_in, pot_ref), (block_ref, raw)))]
+    for load in loads:
+        load.start()
     rows = NJ * NXY // DEGREE
 
     def load_stored(k):
@@ -140,14 +144,16 @@
                 rows_y = side_y[side, p, 4:8] if side == 0 else side_y[side, p, 0:4]
                 beta_y[side, p] = jnp.broadcast_to(rows_y[:, None, :], (CX, ORB, CZ))
 
-    load_block.wait()
+    for load in loads[:3]:
+        load.wait()
+    prepare()
+    loads[3].wait()
     for k in range(DEGREE):
         load_stored(k).start()
 
     for xy in range(NXY):
         field[0, 2 + xy // CY, 2 + xy % CY] = raw[pl.ds(xy, ORB, stride=NXY), :]
     field[1, 2:6, 2:10] = jnp.zeros((CX, CY, ORB, CZ), F32)
-    prepare()
 
     pl.semaphore_wait(barrier, 7 + PLANE - 1 + NG_Z - 1)
 
@@ -158,16 +164,19 @@
                 send_sem=hs_sem.at[slot, n], recv_sem=hr_sem.at[slot, n],
                 device_id=device, device_id_type=MESH)
         own_x, own_y = slice(2, 6), slice(2, 10)
-        return (
+        corners = (
             copy((2, 2), (6, 10), 4, diagonal[0]),
             copy((2, 9), (6, 1), 5, diagonal[1]),
             copy((5, 2), (1, 10), 6, diagonal[2]),
             copy((5, 9), (1, 1), 7, diagonal[3]),
+        )
+        faces = (
             copy((own_x, slice(2, 4)), (own_x, slice(10, 12)), 3, yl),
             copy((own_x, slice(8, 10)), (own_x, slice(0, 2)), 2, yr),
             copy((slice(2, 4), own_y), (slice(6, 8), own_y), 1, xl),
             copy((slice(4, 6), own_y), (slice(0, 2), own_y), 0, xr),
         )
+        return corners, faces
 
     def coef_copies(slot):
         def copy(side, n, device):
@@ -177,9 +186,18 @@
                 device_id=device, device_id_type=MESH)
         return copy(3, 3, yl), copy(2, 2, yr), copy(1, 1, xl), copy(0, 0, xr)
 
+    def wait_sent(slot):
+        corners, faces = halo_copies(slot)
+        for c in corners + faces + coef_copies(slot):
+            c.wait_send()
+
     lanes = lax.broadcasted_iota(jnp.int32, (1, ORB, CZ), 2)
     lane = lax.broadcasted_iota(jnp.int32, (ORB, CZ), 1)
     side_scale = 0.5 / HALF
+
+    def along(cur):
+        zero = jnp.zeros((1, ORB, CZ), F32)
+        return jnp.concatenate([zero, cur[:-1]], axis=0) + jnp.concatenate([cur[1:], zero], axis=0)
 
     def along_z(cur):
         return (jnp.where(lanes == 0, 0.0, pltpu.roll(cur, 1, 2))
@@ -199,11 +217,9 @@
         return total
 
     def first_inside(slot, weights):
-        zero = jnp.zeros((1, ORB, CZ), F32)
         for x in range(CX):
             cur = field[slot, 2 + x, 2:10]
-            near = jnp.concatenate([zero, cur[:-1]], axis=0) + jnp.concatenate([cur[1:], zero], axis=0)
-            near = near + along_z(cur)
+            near = along(cur) + along_z(cur)
             if x > 0:
                 near = near + field[slot, 1 + x, 2:10]
             if x < CX - 1:
@@ -222,7 +238,7 @@
             weights = [got[:, p:p + 1] for p in range(NPROJ)]
             cur = field[slot, at, 2:10]
             near = field[slot, at - 1, 2:10] + field[slot, at + 1, 2:10]
-            near = near + field[slot, at, 1:9] + field[slot, at, 3:11] + along_z(cur)
+            near = near + along(cur) + along_z(cur)
             inner[at - 1, 1:9] = (
                 beta_x[side, NPROJ] * cur - side_scale * near
                 + spread(weights, lambda p: beta_x[side, p]))
@@ -232,12 +248,17 @@
             weights = [got[:, p:p + 1] for p in range(NPROJ)]
             cur = field[slot, 2:6, at]
             near = field[slot, 2:6, at - 1] + field[slot, 2:6, at + 1]
-            near = near + field[slot, 1:5, at] + field[slot, 3:7, at] + along_z(cur)
+            near = near + along(cur) + along_z(cur)
             inner[1:5, at - 1] = (
                 beta_y[side, NPROJ] * cur - side_scale * near
                 + spread(weights, lambda p: beta_y[side, p]))
 
-    def second(slot, ups, stays, backs):
+    def swap(x):
+        return pltpu.make_async_remote_copy(
+            src_ref=field.at[0, 2 + x, 2:10], dst_ref=other.at[x], send_sem=bs_sem.at[x], recv_sem=br_sem.at[x],
+            device_id=twin, device_id_type=MESH)
+
+    def second(slot, ups, stays, backs, last):
         weights = coefficients(inner[1:5, 1:9])
         for x in range(CX):
             cur = inner[1 + x, 1:9]
@@ -247,6 +268,11 @@
             field[1 - slot, 2 + x, 2:10] = (
                 ups * twice + stays * field[slot, 2 + x, 2:10] - backs * field[1 - slot, 2 + x, 2:10])
 
+            if 0 < x < CX - 1:
+                @pl.when(last)
+                def _(x=x):
+                    swap(x).start()
+
     def split_stored(k):
         load_stored(k).wait()
         first = pl.multiple_of(k * (NJ // DEGREE), NJ // DEGREE)
@@ -264,8 +290,8 @@
 
     def step(k, carry):
         slot = lax.rem(k, 2)
-        copies = halo_copies(slot)
-        for c in copies:
+        corners, faces = halo_copies(slot)
+        for c in corners + faces:
             c.start()
 
         @pl.when(k == 0)
@@ -287,8 +313,7 @@
 
         @pl.when(k > 0)
         def _():
-            for c in halo_copies(1 - slot) + coef_copies(1 - slot):
-                c.wait_send()
+            wait_sent(1 - slot)
 
         @pl.when(k == 0)
         def _():
@@ -296,43 +321,51 @@
                 c.wait()
             spread_sides()
 
-        for c in copies + more:
+        for c in faces + more:
             c.wait_recv()
         first_outside(slot)
-        second(slot, pick(k, UPS), pick(k, STAYS), pick(k, BACKS))
+        ups = pick(k, UPS)
+        second(slot, ups, pick(k, STAYS), pick(k, BACKS), k == ROUNDS - 1)
+        for c in corners:
+            c.wait_recv()
+        twice = ups * (2.0 * side_scale * side_scale)
+        for x, y, at_x, at_y in ((2, 2, 1, 1), (2, 9, 1, 10), (5, 2, 6, 1), (5, 9, 6, 10)):
+            field[1 - slot, x, y] = field[1 - slot, x, y] + twice * field[slot, at_x, at_y]
+
+        @pl.when(k == ROUNDS - 1)
+        def _():
+            swap(0).start()
+            swap(CX - 1).start()
+
         return carry
 
     lax.fori_loop(0, ROUNDS, step, 0)
-    for c in halo_copies((ROUNDS - 1) % 2) + coef_copies((ROUNDS - 1) % 2):
-        c.wait_send()
-
-    swap = pltpu.make_async_remote_copy(
-        src_ref=field.at[0, 2:6, 2:10], dst_ref=other, send_sem=b_sem.at[0], recv_sem=b_sem.at[1],
-        device_id=twin, device_id_type=MESH)
-    swap.start()
-    swap.wait()
+    wait_sent((ROUNDS - 1) % 2)
 
     first_core = band == 0
-    for xy in range(NXY):
-        mine, theirs = field[0, 2 + xy // CY, 2 + xy % CY], other[xy // CY, xy % CY]
-        both = jnp.concatenate(
-            [jnp.where(first_core, mine, theirs), jnp.where(first_core, theirs, mine)], axis=0)
-        high = both.astype(BF16)
-        wmat[0:16, xy * CZ:(xy + 1) * CZ] = high
-        wmat[16:32, xy * CZ:(xy + 1) * CZ] = (both - high.astype(F32)).astype(BF16)
-
     def send1(c):
         return pltpu.make_async_remote_copy(
             src_ref=pbuf.at[c], dst_ref=r1.at[mz], send_sem=p1s.at[c], recv_sem=p1r.at[mz],
             device_id=(gx, c * NG_Y + my, band), device_id_type=MESH)
 
     nt = (((1,), (1,)), ((), ()))
+    for step_x, x in enumerate((1, 2, 0, 3)):
+        swap(x).wait_recv()
+        for y in range(CY):
+            mine, theirs = field[0, 2 + x, 2 + y], other[x, y]
+            both = jnp.concatenate(
+                [jnp.where(first_core, mine, theirs), jnp.where(first_core, theirs, mine)], axis=0)
+            high = both.astype(BF16)
+            wmat[0:16, y * CZ:(y + 1) * CZ] = high
+            wmat[16:32, y * CZ:(y + 1) * CZ] = (both - high.astype(F32)).astype(BF16)
+        weights = wmat[...]
+        cols = slice(x * CY * CZ, (x + 1) * CY * CZ)
+        got = lax.dot_general(weights, s_hi[:, cols], nt, preferred_element_type=F32)
+        got = got[0:16] + got[16:32]
+        got = got + lax.dot_general(weights[0:16], s_lo[:, cols], nt, preferred_element_type=F32)
+        total[...] = got if step_x == 0 else total[...] + got
     for t in range(NJ // 128):
-        weights = wmat[...]
-        got = lax.dot_general(s_hi[t * 128:(t + 1) * 128, :], weights, nt, preferred_element_type=F32)
-        got = got + lax.dot_general(s_lo[t * 128:(t + 1) * 128, :], weights, nt, preferred_element_type=F32)
-        flat = got.T
-        flat = flat[0:16] + flat[16:32]
+        flat = total[:, t * 128:(t + 1) * 128]
         for h in range(2):
             c = 2 * t + h
             pbuf[c] = flat[8 * h:8 * h + 8]
@@ -351,6 +384,8 @@
             src_ref=pbuf.at[at], dst_ref=r1.at[at], send_sem=p1s.at[at], recv_sem=p1r.at[at],
             device_id=device, device_id_type=MESH)
 
+    for x in range(CX):
+        swap(x).wait_send()
     for i in range(1, NG_Z):
         recv1(i).wait_recv()
     g2[plane] = jnp.sum(r1[...], axis=0)
@@ -426,8 +461,14 @@
         give(x).wait_send()
 
 
+def finish(a_ref, b_ref, a_out, b_out):
+    a_out[...] = a_ref[...]
+    b_out[...] = b_ref[...]
+
+
 def on_device(block, potential, proj_index, proj_value, proj_strength, stored):
     vmem = pl.BlockSpec(memory_space=pltpu.VMEM)
+    hbm = pl.BlockSpec(memory_space=pltpu.HBM)
     dma = pltpu.SemaphoreType.DMA
     projected, intersection = pl.pallas_call(
         kernel,
@@ -436,13 +477,15 @@
             jax.ShapeDtypeStruct((2 * ORB, NJ), F32),
         ),
         in_specs=[
-            pl.BlockSpec(memory_space=pl.ANY), vmem, vmem, vmem,
-            pl.BlockSpec(memory_space=pltpu.SMEM), pl.BlockSpec(memory_space=pl.ANY)],
+            hbm, hbm, hbm, hbm, pl.BlockSpec(memory_space=pltpu.SMEM), hbm],
         out_specs=(vmem, vmem),
         scratch_shapes=[
             pltpu.VMEM((2, CX + 4, CY + 4, ORB, CZ), F32),
             pltpu.VMEM((CX + 2, CY + 2, ORB, CZ), F32),
             pltpu.VMEM((ORB * NXY, CZ), F32),
+            pltpu.VMEM((NXY, CZ), F32),
+            pltpu.VMEM((NPROJ, 128), jnp.int32),
+            pltpu.VMEM((NPROJ, 128), F32),
             pltpu.VMEM((NPROJ + 1, CX, CY, ORB, CZ), F32),
             pltpu.VMEM((NPROJ + 1, NXY, CZ), F32),
             pltpu.VMEM((NPROJ + 1, 2 * CX, CZ), F32),
@@ -456,14 +499,15 @@
             pltpu.VMEM((NJ, CELLS), BF16),
             pltpu.VMEM((NJ, CELLS), BF16),
             pltpu.VMEM((CX, CY, ORB, CZ), F32),
-            pltpu.VMEM((4 * ORB, CELLS), BF16),
+            pltpu.VMEM((4 * ORB, CY * CZ), BF16),
+            pltpu.VMEM((2 * ORB, NJ), F32),
             pltpu.VMEM((NG_Z, ORB, CZ), F32),
             pltpu.VMEM((NG_Z, ORB, CZ), F32),
             pltpu.VMEM((PLANE, ORB, CZ), F32),
             pltpu.VMEM((NG_Z, ORB, CZ), F32),
             pltpu.VMEM((CX, CY, ORB, CZ), F32),
             pltpu.VMEM((CX, CY, ORB, CZ), F32),
-            dma, dma((DEGREE,)), dma((2, 12)), dma((2, 12)), dma((4,)), dma((4,)), dma((2,)),
+            dma((4,)), dma((DEGREE,)), dma((2, 12)), dma((2, 12)), dma((4,)), dma((4,)), dma((CX,)), dma((CX,)),
             dma((NG_Z,)), dma((NG_Z,)), dma((PLANE,)), dma((PLANE,)), dma((NG_Z,)), dma((NG_Z,)),
             dma((CX,)), dma((CX,)),
         ],
@@ -473,6 +517,13 @@
     )(
         block.reshape(ORB * NXY, CZ), potential.reshape(NXY, CZ), proj_index, proj_value,
         proj_strength, stored.reshape(NJ * NXY, CZ))
+    projected, intersection = pl.pallas_call(
+        finish,
+        out_shape=(jax.ShapeDtypeStruct(projected.shape, F32), jax.ShapeDtypeStruct(intersection.shape, F32)),
+        in_specs=[vmem, vmem],
+        out_specs=(vmem, vmem),
+        name="finish",
+    )(projected, intersection)
     return projected.reshape(block.shape), intersection.T
 
 

time: 61.8 us -> 56.7 us (0.917)
  local copies, waits for them, and re-layouts: 2.94 us -> 0 us
  Pallas kernels: 58 us -> 55.9 us
    pallas_call x1, Pallas kernels: 58 us -> 54.3 us  [on_device(): pl.pallas_call(kernel, out_shape=(jax.ShapeDtypeStruct((ORB * NXY, CZ), F...]
    unnamed x2 -> x0, local copies, waits for them, and re-layouts: 2.94 us -> none
    pallas_call x0 -> x1, Pallas kernels: none -> 1.57 us  [on_device(): pl.pallas_call(finish, out_shape=(jax.ShapeDtypeStruct(projected.shape, F...]
where the time goes in v3:
time: 56.7 us; the launch traced here: 56.5 us
  Pallas kernels  55.9 us (99%)
  between operations  0.64 us (1%)
    pallas_call x1, Pallas kernels, on_device(): pl.pallas_call(kernel, out_shape=(jax.ShapeDtypeStruct((ORB * NXY, CZ), F...  54.3 us
    pallas_call x1, Pallas kernels, on_device(): pl.pallas_call(finish, out_shape=(jax.ShapeDtypeStruct(projected.shape, F...  1.57 us

profile of v3, /device:TPU:1, one launch (start us, length us, event | category | flops | bytes accessed | tf_op | source)
XLA Modules:
  0.0 56.5 jit_solution(4243718384015195846)
XLA Ops:
  0.6 54.3 %filter_project.1 = (f32[256,128]{1,0:T(8,128)}, f32[16,512]{1,0:T(8,128)}) custom-call(f32[256,128]{1,0:T(8,128)} %bitcast.6, f32[32,128]{1,0:T(8,128)} %bitcast.7, s32[8,128]{1,0:T(8,128)} %idx_in.1, f32[8,128]{1,0:T(8,128)} %val_in.1, f32[8]{0:T(128)} %str_ref.1, f32[16384,128]{1,0:T(8,128)} %bitcast.5), custom_call_target="tpu_custom_call" | custom-call | tf_op jit(solution)/shard_map/filter_project/pallas_call | solution.py:473
  55.0 1.6 %finish.1 = (f32[256,128]{1,0:T(8,128)}, f32[16,512]{1,0:T(8,128)}) custom-call(f32[256,128]{1,0:T(8,128)} %get-tuple-element.6.a_ref, f32[16,512]{1,0:T(8,128)} %get-tuple-element.7.b_ref), custom_call_target="tpu_custom_call" | custom-call | tf_op jit(solution)/shard_map/finish/pallas_call | solution.py:520

commit v4 on v3

v4 whole, which is shorter than its diff:
```python
import functools

import jax
import jax.numpy as jnp
from jax import lax
from jax.experimental import pallas as pl
from jax.experimental.pallas import tpu as pltpu
from jax.sharding import PartitionSpec as P

DEGREE = 8
LOW_EDGE = 0.0
CUT_EDGE = 1.0
TOP_EDGE = 10.0
HALF = (TOP_EDGE - CUT_EDGE) / 2.0
CENTER = (TOP_EDGE + CUT_EDGE) / 2.0

MESH = pl.DeviceIdType.MESH
F32 = jnp.float32
BF16 = jnp.bfloat16

CX, CY, CZ = 4, 8, 128
NXY = CX * CY
CELLS = NXY * CZ
ORB = 8
NPROJ = 8
NJ = 512
NG_X, NG_Y, NG_Z = 4, 4, 8
PLANE = NG_X * NG_Y


def chebyshev_at_low():
    x = (LOW_EDGE - CENTER) / HALF
    t = [1.0, x]
    while len(t) <= DEGREE:
        t.append(2.0 * x * t[-1] - t[-2])
    return t


AT_LOW = chebyshev_at_low()


def kernel(
    block_ref, pot_in, idx_in, val_in, str_in, stored_ref,
    out_ref, int_ref,
    field, inner, inner2, raw, pot_ref, idx_ref, val_ref, str_ref, beta, dense, edge, nook, side_x, side_y, side_d,
    beta_x, beta_y, beta_d, coef, coef_in, part, part_in, sraw, s_hi, s_lo, other, wmat, total,
    pbuf, r1, g2, q3, fix, csend, crecv,
    in_sem, st_sem, hs_sem, hr_sem, fs_sem, fr_sem, bs_sem, br_sem, p1s, p1r, p2s, p2r, p3s, p3r, cs_sem, cr_sem,
):
    gx = lax.axis_index("gx")
    gyz = lax.axis_index("gyz")
    band = lax.axis_index("band")
    mz = lax.div(gyz, NG_Y)
    my = lax.rem(gyz, NG_Y)
    plane = gx * NG_Y + my
    left, right = lax.rem(gx + NG_X - 1, NG_X), lax.rem(gx + 1, NG_X)
    down, up = lax.rem(gyz + NG_Y * NG_Z - 1, NG_Y * NG_Z), lax.rem(gyz + 1, NG_Y * NG_Z)
    xl, xr, yl, yr = (left, gyz, band), (right, gyz, band), (gx, down, band), (gx, up, band)
    diagonal = [(x, y, band) for x in (left, right) for y in (down, up)]
    x2 = (lax.rem(gx + 2, NG_X), gyz, band)
    down2 = (gx, lax.rem(gyz + NG_Y * NG_Z - 2, NG_Y * NG_Z), band)
    up2 = (gx, lax.rem(gyz + 2, NG_Y * NG_Z), band)
    twin = (gx, gyz, 1 - band)

    def plane_peer(i):
        at = lax.rem(plane + i, PLANE)
        return at, (lax.div(at, NG_Y), mz * NG_Y + lax.rem(at, NG_Y), band)

    def z_peer(i):
        at = lax.rem(mz + i, NG_Z)
        return at, (gx, at * NG_Y + my, band)

    barrier = pltpu.get_barrier_semaphore()

    def greet(device):
        pl.semaphore_signal(barrier, inc=1, device_id=device, device_id_type=MESH)

    for device in diagonal + [yl, yr, down2, up2, twin]:
        greet(device)
    for i in range(1, PLANE):
        greet(plane_peer(i)[1])
    for i in range(1, NG_Z):
        greet(z_peer(i)[1])

    loads = [
        pltpu.make_async_copy(src, dst, in_sem.at[n])
        for n, (src, dst) in enumerate(
            ((idx_in, idx_ref), (val_in, val_ref), (pot_in, pot_ref), (str_in, str_ref), (block_ref, raw)))]
    for load in loads:
        load.start()
    def load_stored(xy):
        return pltpu.make_async_copy(stored_ref.at[:, xy], sraw.at[xy], st_sem.at[xy])


    def prepare():
        edge[...] = jnp.zeros(edge.shape, F32)
        nook[...] = jnp.zeros(nook.shape, F32)
        low_edge = lax.broadcasted_iota(jnp.int32, (NXY, 128), 0)
        at_row = lax.broadcasted_iota(jnp.int32, (CZ, 128), 0)
        for p in range(NPROJ):
            index = idx_ref[p:p + 1, :]
            value = val_ref[p:p + 1, :] * jnp.sqrt(jnp.full((1, 128), str_ref[p] * (1.0 / HALF), F32))
            v1 = value.astype(BF16).astype(F32)
            v2 = (value - v1).astype(BF16).astype(F32)
            v3 = value - v1 - v2
            at_xy = low_edge == lax.shift_right_logical(index, 7)
            at_z = at_row == lax.bitwise_and(index, 127)
            picks = jnp.concatenate([jnp.where(at_xy, v, 0.0) for v in (v1, v2, v3)], axis=0).astype(BF16)
            places = jnp.where(at_z, 1.0, 0.0).astype(BF16)
            got = lax.dot_general(picks, places, (((1,), (1,)), ((), ())), preferred_element_type=F32)
            dense[p] = got[0:NXY] + got[NXY:2 * NXY] + got[2 * NXY:]
        dense[NPROJ] = (pot_ref[...] + (3.0 - CENTER)) * (1.0 / HALF)
        for p in range(NPROJ + 1):
            beta[p] = jnp.broadcast_to(dense[p][:, None, :], (NXY, ORB, CZ)).reshape(CX, CY, ORB, CZ)
            for layer in range(2):
                for side, y in ((0, layer), (1, CY - 1 - layer)):
                    edge[layer, side, CX * p:CX * p + CX] = dense[p, pl.ds(y, CX, stride=CY), :]
            for n, row in enumerate((0, CY - 1, NXY - CY, NXY - 1)):
                nook[n, p:p + 1] = dense[p, row:row + 1]

    def side_copies(layer):
        def copy(src, dst, n, device):
            return pltpu.make_async_remote_copy(
                src_ref=src, dst_ref=dst, send_sem=fs_sem.at[4 * layer + n], recv_sem=fr_sem.at[4 * layer + n],
                device_id=device, device_id_type=MESH)

        def x_rows(plane):
            return slice(CY * plane, CY * plane + CY)

        return (
            copy(edge.at[layer, 0], side_y.at[1, layer], 3, yl),
            copy(edge.at[layer, 1], side_y.at[0, layer], 2, yr),
            copy(dense.at[:, x_rows(layer)], side_x.at[1, :, x_rows(layer)], 1, xl),
            copy(dense.at[:, x_rows(CX - 1 - layer)], side_x.at[0, :, x_rows(1 - layer)], 0, xr),
        )

    def diagonal_copies():
        def copy(n):
            return pltpu.make_async_remote_copy(
                src_ref=nook.at[n], dst_ref=side_d.at[3 - n], send_sem=fs_sem.at[8 + n], recv_sem=fr_sem.at[8 + n],
                device_id=diagonal[n], device_id_type=MESH)
        return copy(0), copy(1), copy(2), copy(3)

    def spread_sides(layer):
        for p in range(NPROJ + 1):
            for side in range(2):
                n = layer if side == 1 else 1 - layer
                got = side_x[side, p, CY * n:CY * n + CY]
                beta_x[side, p, n] = jnp.broadcast_to(got[:, None, :], (CY, ORB, CZ))
                got = side_y[side, layer, CX * p:CX * p + CX]
                beta_y[side, p, :, n] = jnp.broadcast_to(got[:, None, :], (CX, ORB, CZ))

    def spread_diagonals():
        for p in range(NPROJ + 1):
            for n in range(4):
                beta_d[n, p] = jnp.broadcast_to(side_d[n, p:p + 1], (ORB, CZ))

    for xy in range(NXY):
        load_stored(xy).start()
    for load in loads[:4]:
        load.wait()
    prepare()
    loads[4].wait()

    for xy in range(NXY):
        field[0, 3 + xy // CY, 3 + xy % CY] = raw[pl.ds(xy, ORB, stride=NXY), :]

    def split_stored(k):
        def part(n, carry):
            xy = 4 * k + n
            load_stored(xy).wait()
            got = sraw[xy]
            high = got.astype(BF16)
            cols = pl.ds(pl.multiple_of(xy * CZ, CZ), CZ)
            s_hi[:, cols] = high
            s_lo[:, cols] = (got - high.astype(F32)).astype(BF16)
            return carry

        lax.fori_loop(0, 4, part, 0)

    pl.semaphore_wait(barrier, 9 + PLANE - 1 + NG_Z - 1)

    def halo_copies(slot, depth):
        def copy(src, dst, n, device):
            return pltpu.make_async_remote_copy(
                src_ref=field.at[(slot,) + src], dst_ref=field.at[(slot,) + dst],
                send_sem=hs_sem.at[slot, n], recv_sem=hr_sem.at[slot, n],
                device_id=device, device_id_type=MESH)
        own_x, own_y = slice(3, 7), slice(3, 11)
        low, high, n = 3, 3 + CX, depth - 1
        low_y, high_y = 3, 3 + CY
        x_low, x_high, y_low, y_high = (
            slice(low, low + n), slice(high - n, high), slice(low_y, low_y + n), slice(high_y - n, high_y))
        x_over, x_under, y_over, y_under = (
            slice(high, high + n), slice(low - n, low), slice(high_y, high_y + n), slice(low_y - n, low_y))
        corners = (
            copy((x_low, y_low), (x_over, y_over), 4, diagonal[0]),
            copy((x_low, y_high), (x_over, y_under), 5, diagonal[1]),
            copy((x_high, y_low), (x_under, y_over), 6, diagonal[2]),
            copy((x_high, y_high), (x_under, y_under), 7, diagonal[3]),
        )
        faces_y = (
            copy((own_x, slice(3, 3 + depth)), (own_x, slice(11, 11 + depth)), 3, yl),
            copy((own_x, slice(11 - depth, 11)), (own_x, slice(3 - depth, 3)), 2, yr),
        )
        faces_x = (
            copy((slice(3, 3 + depth), own_y), (slice(7, 7 + depth), own_y), 1, xl),
            copy((slice(7 - depth, 7), own_y), (slice(3 - depth, 3), own_y), 0, xr),
        )
        return corners, faces_y, faces_x

    def coef_copies(slot, count):
        def copy(place, device):
            return pltpu.make_async_remote_copy(
                src_ref=coef.at[slot], dst_ref=coef_in.at[slot, place],
                send_sem=hs_sem.at[slot, 8 + place], recv_sem=hr_sem.at[slot, 8 + place],
                device_id=device, device_id_type=MESH)
        return [copy(place, device) for place, device in (
            (7, diagonal[0]), (6, diagonal[1]), (5, diagonal[2]), (4, diagonal[3]),
            (10, down2), (9, up2), (8, x2), (3, yl), (2, yr), (1, xl), (0, xr))[11 - count:]]

    def part_copies(slot):
        def copy(place, device):
            return pltpu.make_async_remote_copy(
                src_ref=part.at[slot], dst_ref=part_in.at[slot, place],
                send_sem=hs_sem.at[slot, 19 + place], recv_sem=hr_sem.at[slot, 19 + place],
                device_id=device, device_id_type=MESH)
        return [copy(place, device) for place, device in ((3, yl), (2, yr), (1, xl), (0, xr))]

    lanes = lax.broadcasted_iota(jnp.int32, (1, ORB, CZ), 2)
    lane = lax.broadcasted_iota(jnp.int32, (ORB, CZ), 1)
    side_scale = 0.5 / HALF

    def along(cur):
        zero = jnp.zeros((1, ORB, CZ), F32)
        return jnp.concatenate([zero, cur[:-1]], axis=0) + jnp.concatenate([cur[1:], zero], axis=0)

    def along_z(cur):
        return (jnp.where(lanes == 0, 0.0, pltpu.roll(cur, 1, cur.ndim - 1))
                + jnp.where(lanes == CZ - 1, 0.0, pltpu.roll(cur, CZ - 1, cur.ndim - 1)))

    def dot_tiles(values, tiles):
        return [jnp.sum(jnp.sum(values * tiles(p), axis=tuple(range(values.ndim - 2))), axis=1, keepdims=True)
                for p in range(NPROJ)]

    def pack(columns):
        packed = jnp.zeros((ORB, CZ), F32)
        for n, column in enumerate(columns):
            packed = jnp.where(lane == n, column, packed)
        return packed

    def unpack(tile):
        return [tile[:, p:p + 1] for p in range(NPROJ)]

    def spread(weights, tiles):
        total = weights[0] * tiles(0)
        for p in range(1, NPROJ):
            total = total + weights[p] * tiles(p)
        return total

    def own_coefficients(values):
        return dot_tiles(values, lambda p: beta[p])

    def inside(slot, weights, x):
        cur = field[slot, 3 + x, 3:11]
        near = along(cur) + along_z(cur)
        if x > 0:
            near = near + field[slot, 2 + x, 3:11]
        if x < CX - 1:
            near = near + field[slot, 4 + x, 3:11]
        return beta[NPROJ, x] * cur - side_scale * near + spread(weights, lambda p: beta[p, x])

    def add_halo(slot):
        inner[2, 2:10] = inner[2, 2:10] - side_scale * field[slot, 2, 3:11]
        inner[5, 2:10] = inner[5, 2:10] - side_scale * field[slot, 7, 3:11]
        inner[2:6, 2] = inner[2:6, 2] - side_scale * field[slot, 3:7, 2]
        inner[2:6, 9] = inner[2:6, 9] - side_scale * field[slot, 3:7, 11]

    def first_layer(slot):
        for side, at in ((0, 2), (1, 7)):
            cur = field[slot, at, 3:11]
            near = field[slot, at - 1, 3:11] + field[slot, at + 1, 3:11] + along(cur) + along_z(cur)
            inner[at - 1, 2:10] = (
                beta_x[side, NPROJ, 1 - side] * cur - side_scale * near
                + spread(unpack(coef_in[slot, side]), lambda p: beta_x[side, p, 1 - side]))
        for side, at in ((0, 2), (1, 11)):
            cur = field[slot, 3:7, at]
            near = field[slot, 3:7, at - 1] + field[slot, 3:7, at + 1] + along(cur) + along_z(cur)
            inner[2:6, at - 1] = (
                beta_y[side, NPROJ, :, 1 - side] * cur - side_scale * near
                + spread(unpack(coef_in[slot, 2 + side]), lambda p: beta_y[side, p, :, 1 - side]))

    def own_x_of_inner(x, weights):
        cur = inner[2 + x, 2:10]
        near = inner[1 + x, 2:10] + inner[3 + x, 2:10] + inner[2 + x, 1:9] + inner[2 + x, 3:11]
        near = near + along_z(cur)
        return beta[NPROJ, x] * cur - side_scale * near + spread(weights, lambda p: beta[p, x])

    def degree_two():
        weights = own_coefficients(inner[2:6, 2:10])
        for x in range(CX):
            field[1, 3 + x, 3:11] = (
                (2.0 / AT_LOW[2]) * own_x_of_inner(x, weights) - (1.0 / AT_LOW[2]) * field[0, 3 + x, 3:11])

    def outer_layers(slot):
        for side, at in ((0, 1), (1, 7)):
            cur = field[slot, at:at + 2, 3:11]
            near = field[slot, at - 1:at + 1, 3:11] + field[slot, at + 1:at + 3, 3:11] + along_z(cur)
            near = near + field[slot, at:at + 2, 2:10] + field[slot, at:at + 2, 4:12]
            inner[at - 1:at + 1, 2:10] = (
                beta_x[side, NPROJ] * cur - side_scale * near
                + spread(unpack(coef_in[slot, side]), lambda p: beta_x[side, p]))
        for side, at in ((0, 1), (1, 11)):
            cur = field[slot, 3:7, at:at + 2]
            near = field[slot, 3:7, at - 1:at + 1] + field[slot, 3:7, at + 1:at + 3] + along_z(cur)
            near = near + field[slot, 2:6, at:at + 2] + field[slot, 4:8, at:at + 2]
            inner[2:6, at - 1:at + 1] = (
                beta_y[side, NPROJ] * cur - side_scale * near
                + spread(unpack(coef_in[slot, 2 + side]), lambda p: beta_y[side, p]))
        for n, (x, y) in enumerate(((2, 2), (2, 11), (7, 2), (7, 11))):
            cur = field[slot, x, y]
            near = field[slot, x - 1, y] + field[slot, x + 1, y] + field[slot, x, y - 1] + field[slot, x, y + 1]
            near = near + along_z(cur[None])[0]
            inner[x - 1, y - 1] = (
                beta_d[n, NPROJ] * cur - side_scale * near
                + spread(unpack(coef_in[slot, 4 + n]), lambda p: beta_d[n, p]))

    XL, XR, YL, YR = 1, 2, 3, 4

    def group(tile, n):
        return pltpu.roll(tile, CZ - 8 * n, 1)

    def next_coefficients(slot):
        got = [coef_in[slot, place] for place in range(11)]
        mine = coef[slot]
        own = group(got[0], XR) + group(got[1], XL) + group(got[2], YR) + group(got[3], YL)
        low_x = group(mine, XL) + group(got[8], XR) + group(got[4], YR) + group(got[5], YL)
        high_x = group(mine, XR) + group(got[8], XL) + group(got[6], YR) + group(got[7], YL)
        low_y = group(mine, YL) + group(got[9], YR) + group(got[4], XR) + group(got[6], XL)
        high_y = group(mine, YR) + group(got[10], YL) + group(got[5], XR) + group(got[7], XL)
        out = [unpack(part[slot] - side_scale * own)]
        for place, terms in enumerate((low_x, high_x, low_y, high_y)):
            out.append(unpack(part_in[slot, place] - side_scale * terms))
        return out

    def middle(slot, weights):
        for x in range(CX):
            inner2[1 + x, 1:9] = 2.0 * own_x_of_inner(x, weights[0]) - field[slot, 3 + x, 3:11]
        for side, at in ((0, 1), (1, 6)):
            cur = inner[at, 2:10]
            near = inner[at - 1, 2:10] + inner[at + 1, 2:10] + inner[at, 1:9] + inner[at, 3:11] + along_z(cur)
            got = (beta_x[side, NPROJ, 1 - side] * cur - side_scale * near
                   + spread(weights[1 + side], lambda p: beta_x[side, p, 1 - side]))
            inner2[at - 1, 1:9] = 2.0 * got - field[slot, at + 1, 3:11]
        for side, at in ((0, 1), (1, 10)):
            cur = inner[2:6, at]
            near = inner[2:6, at - 1] + inner[2:6, at + 1] + inner[1:5, at] + inner[3:7, at] + along_z(cur)
            got = (beta_y[side, NPROJ, :, 1 - side] * cur - side_scale * near
                   + spread(weights[3 + side], lambda p: beta_y[side, p, :, 1 - side]))
            inner2[1:5, at - 1] = 2.0 * got - field[slot, 3:7, at + 1]

    def swap(x):
        return pltpu.make_async_remote_copy(
            src_ref=field.at[1, 3 + x, 3:11], dst_ref=other.at[x], send_sem=bs_sem.at[x], recv_sem=br_sem.at[x],
            device_id=twin, device_id_type=MESH)

    def degree_three(slot, scale, back, last):
        weights = own_coefficients(inner2[1:5, 1:9])
        for x in range(CX):
            cur = inner2[1 + x, 1:9]
            near = inner2[x, 1:9] + inner2[2 + x, 1:9] + inner2[1 + x, 0:8] + inner2[1 + x, 2:10]
            near = near + along_z(cur)
            got = beta[NPROJ, x] * cur - side_scale * near + spread(weights, lambda p: beta[p, x])
            got = 2.0 * got - inner[2 + x, 2:10]
            field[1 - slot, 3 + x, 3:11] = scale * got - back * field[1 - slot, 3 + x, 3:11]

            @pl.when(last)
            def _(x=x):
                swap(x).start()

    def wait_sent(slot):
        corners, faces_y, faces_x = halo_copies(slot, 3)
        for c in corners + faces_y + faces_x + tuple(coef_copies(slot, 11)) + tuple(part_copies(slot)):
            c.wait_send()

    def start(copies):
        for c in copies:
            c.start()

    corners, faces_y, faces_x = halo_copies(0, 2)
    start(corners + faces_y)
    weights = own_coefficients(field[0, 3:7, 3:11])
    coef[0] = pack(weights)
    tiles = coef_copies(0, 4)
    start(tiles)
    near_sides, next_sides, far_sides = side_copies(0), side_copies(1), diagonal_copies()
    start(near_sides[:2])
    start(faces_x)
    start(near_sides[2:])
    for x in range(CX):
        inner[2 + x, 2:10] = inside(0, weights, x)
    split_stored(0)
    start(next_sides + far_sides)
    split_stored(1)
    for c in near_sides:
        c.wait_recv()
    spread_sides(0)
    for c in faces_x + faces_y + tuple(tiles):
        c.wait_recv()
    add_halo(0)
    first_layer(0)
    degree_two()
    for c in corners:
        c.wait_recv()
    twice = (2.0 / AT_LOW[2]) * (2.0 * side_scale * side_scale)
    for x, y, at_x, at_y in ((3, 3, 2, 2), (3, 10, 2, 11), (6, 3, 7, 2), (6, 10, 7, 11)):
        field[1, x, y] = field[1, x, y] + twice * field[0, at_x, at_y]

    def step(k, carry):
        slot = 1 - k
        corners, faces_y, faces_x = halo_copies(slot, 3)
        start(corners)
        weights = own_coefficients(field[slot, 3:7, 3:11])
        columns = list(weights)
        for side, at in ((0, 3), (1, 6)):
            columns += dot_tiles(field[slot, at, 3:11], lambda p: beta_x[side, p, 1 - side])
        for side, at in ((0, 3), (1, 10)):
            columns += dot_tiles(field[slot, 3:7, at], lambda p: beta_y[side, p, :, 1 - side])
        coef[slot] = pack(columns)
        tiles = coef_copies(slot, 11)
        start(tiles)
        start(faces_y)

        @pl.when(k == 0)
        def _():
            corners, faces_y, faces_x = halo_copies(0, 2)
            for c in corners + faces_y + faces_x + tuple(coef_copies(0, 4)):
                c.wait_send()
            field[0, 3:7, 3:11] = inner[2:6, 2:10]

        for x in range(CX):
            inner[2 + x, 2:10] = inside(slot, weights, x)
        part[slot] = pack(own_coefficients(inner[2:6, 2:10]))
        parts = part_copies(slot)
        start(parts[:2])
        start(faces_x)
        start(parts[2:])

        @pl.when(k == 0)
        def _():
            for c in near_sides + next_sides + far_sides:
                c.wait_send()
            for c in next_sides + far_sides:
                c.wait_recv()
            spread_sides(1)
            spread_diagonals()

        for n in range(3):
            split_stored(2 + 3 * k + n)

        @pl.when(k == 1)
        def _():
            wait_sent(1)

        for c in faces_x + faces_y + tuple(tiles) + tuple(parts) + corners:
            c.wait_recv()
        add_halo(slot)
        outer_layers(slot)
        middle(slot, next_coefficients(slot))
        scale = jnp.where(k == 0, 2.0 * AT_LOW[2] / AT_LOW[5], 2.0 * AT_LOW[5] / AT_LOW[8])
        back = jnp.where(k == 0, 1.0 / AT_LOW[5], AT_LOW[2] / AT_LOW[8])
        degree_three(slot, scale, back, k == 1)
        return carry

    lax.fori_loop(0, 2, step, 0)
    wait_sent(0)

    first_core = band == 0
    def send1(c):
        return pltpu.make_async_remote_copy(
            src_ref=pbuf.at[c], dst_ref=r1.at[mz], send_sem=p1s.at[c], recv_sem=p1r.at[mz],
            device_id=(gx, c * NG_Y + my, band), device_id_type=MESH)

    nt = (((1,), (1,)), ((), ()))
    for x in range(CX):
        swap(x).wait_recv()
        for y in range(CY):
            mine, theirs = field[1, 3 + x, 3 + y], other[x, y]
            both = jnp.concatenate(
                [jnp.where(first_core, mine, theirs), jnp.where(first_core, theirs, mine)], axis=0)
            high = both.astype(BF16)
            wmat[0:16, y * CZ:(y + 1) * CZ] = high
            wmat[16:32, y * CZ:(y + 1) * CZ] = (both - high.astype(F32)).astype(BF16)
        weights = wmat[...]
        cols = slice(x * CY * CZ, (x + 1) * CY * CZ)
        got = lax.dot_general(weights, s_hi[:, cols], nt, preferred_element_type=F32)
        got = got[0:16] + got[16:32]
        got = got + lax.dot_general(weights[0:16], s_lo[:, cols], nt, preferred_element_type=F32)
        total[...] = got if x == 0 else total[...] + got
    for t in range(NJ // 128):
        flat = total[:, t * 128:(t + 1) * 128]
        for h in range(2):
            c = 2 * t + h
            pbuf[c] = flat[8 * h:8 * h + 8]

            @pl.when(mz == c)
            def _(c=c):
                r1[c] = pbuf[c]

            @pl.when(mz != c)
            def _(c=c):
                send1(c).start()

    def recv1(i):
        at, device = z_peer(i)
        return pltpu.make_async_remote_copy(
            src_ref=pbuf.at[at], dst_ref=r1.at[at], send_sem=p1s.at[at], recv_sem=p1r.at[at],
            device_id=device, device_id_type=MESH)

    for x in range(CX):
        swap(x).wait_send()
    for i in range(1, NG_Z):
        recv1(i).wait_recv()
    g2[plane] = jnp.sum(r1[...], axis=0)

    def send2(i):
        return pltpu.make_async_remote_copy(
            src_ref=g2.at[plane], dst_ref=g2.at[plane], send_sem=p2s.at[i], recv_sem=p2r.at[plane],
            device_id=plane_peer(i)[1], device_id_type=MESH)

    def recv2(i):
        at, device = plane_peer(i)
        return pltpu.make_async_remote_copy(
            src_ref=g2.at[plane], dst_ref=g2.at[at], send_sem=p2s.at[i], recv_sem=p2r.at[at],
            device_id=device, device_id_type=MESH)

    for i in range(1, PLANE):
        send2(i).start()
    for i in range(1, NG_Z):
        recv1(i).wait_send()
    for i in range(1, PLANE):
        recv2(i).wait_recv()
    q3[mz] = jnp.sum(g2[...], axis=0)

    def send3(i):
        return pltpu.make_async_remote_copy(
            src_ref=q3.at[mz], dst_ref=q3.at[mz], send_sem=p3s.at[i], recv_sem=p3r.at[mz],
            device_id=z_peer(i)[1], device_id_type=MESH)

    for i in range(1, NG_Z):
        send3(i).start()
    for i in range(1, PLANE):
        send2(i).wait_send()
    nn = (((1,), (0,)), ((), ()))

    def arrived(c):
        pltpu.make_async_remote_copy(
            src_ref=q3.at[mz], dst_ref=q3.at[c], send_sem=p3s.at[0], recv_sem=p3r.at[c],
            device_id=(gx, c * NG_Y + my, band), device_id_type=MESH).wait_recv()

    def give(x):
        return pltpu.make_async_remote_copy(
            src_ref=csend.at[x], dst_ref=crecv.at[x], send_sem=cs_sem.at[x], recv_sem=cr_sem.at[x],
            device_id=twin, device_id_type=MESH)

    pairs = NG_Z // 2
    for n, ahead in enumerate((0, 1, 3, 2)):
        pair = lax.rem(lax.div(mz, 2) + ahead, pairs)
        for h in range(2):
            @pl.when(2 * pair + h != mz)
            def _(h=h):
                arrived(2 * pair + h)

        whole = jnp.concatenate([q3[2 * pair], q3[2 * pair + 1]], axis=0)
        rows_j = pl.ds(pl.multiple_of(pair * 128, 128), 128)
        int_ref[:, rows_j] = whole
        high = whole.astype(BF16)
        low = (whole - high.astype(F32)).astype(BF16)
        left_side = jnp.concatenate([high, low], axis=0)
        for x in range(CX):
            cols = slice(x * CY * CZ, (x + 1) * CY * CZ)
            got = lax.dot_general(left_side, s_hi[rows_j, cols], nn, preferred_element_type=F32)
            more = lax.dot_general(high, s_lo[rows_j, cols], nn, preferred_element_type=F32)
            got = got[0:16] + got[16:32] + more
            if n > 0:
                got = got + fix[:, cols]
            if n < pairs - 1:
                fix[:, cols] = got
                continue
            keep = jnp.where(first_core, got[0:8], got[8:16])
            send = jnp.where(first_core, got[8:16], got[0:8])
            for y in range(CY):
                csend[x, y] = send[:, y * CZ:(y + 1) * CZ]
                field[0, 3 + x, 3 + y] = field[1, 3 + x, 3 + y] - keep[:, y * CZ:(y + 1) * CZ]
            give(x).start()
    for i in range(1, NG_Z):
        send3(i).wait_send()
    for x in range(CX):
        give(x).wait_recv()
        for y in range(CY):
            out_ref[pl.ds(x * CY + y, ORB, stride=NXY), :] = field[0, 3 + x, 3 + y] - crecv[x, y]
    for x in range(CX):
        give(x).wait_send()


def finish(a_ref, b_ref, a_out, b_out):
    a_out[...] = a_ref[...]
    b_out[...] = b_ref[...]


def on_device(block, potential, proj_index, proj_value, proj_strength, stored):
    vmem = pl.BlockSpec(memory_space=pltpu.VMEM)
    hbm = pl.BlockSpec(memory_space=pltpu.HBM)
    dma = pltpu.SemaphoreType.DMA
    projected, intersection = pl.pallas_call(
        kernel,
        out_shape=(
            jax.ShapeDtypeStruct((ORB * NXY, CZ), F32),
            jax.ShapeDtypeStruct((2 * ORB, NJ), F32),
        ),
        in_specs=[
            hbm, hbm, hbm, hbm, hbm, hbm],
        out_specs=(vmem, vmem),
        scratch_shapes=[
            pltpu.VMEM((2, CX + 6, CY + 6, ORB, CZ), F32),
            pltpu.VMEM((CX + 4, CY + 4, ORB, CZ), F32),
            pltpu.VMEM((CX + 2, CY + 2, ORB, CZ), F32),
            pltpu.VMEM((ORB * NXY, CZ), F32),
            pltpu.VMEM((NXY, CZ), F32),
            pltpu.VMEM((NPROJ, 128), jnp.int32),
            pltpu.VMEM((NPROJ, 128), F32),
            pltpu.SMEM((NPROJ,), F32),
            pltpu.VMEM((NPROJ + 1, CX, CY, ORB, CZ), F32),
            pltpu.VMEM((NPROJ + 1, NXY, CZ), F32),
            pltpu.VMEM((2, 2, 40, CZ), F32),
            pltpu.VMEM((4, 16, CZ), F32),
            pltpu.VMEM((2, NPROJ + 1, 2 * CY, CZ), F32),
            pltpu.VMEM((2, 2, 40, CZ), F32),
            pltpu.VMEM((4, 16, CZ), F32),
            pltpu.VMEM((2, NPROJ + 1, 2, CY, ORB, CZ), F32),
            pltpu.VMEM((2, NPROJ + 1, CX, 2, ORB, CZ), F32),
            pltpu.VMEM((4, NPROJ + 1, ORB, CZ), F32),
            pltpu.VMEM((2, ORB, CZ), F32),
            pltpu.VMEM((2, 11, ORB, CZ), F32),
            pltpu.VMEM((2, ORB, CZ), F32),
            pltpu.VMEM((2, 4, ORB, CZ), F32),
            pltpu.VMEM((NXY, NJ, CZ), F32),
            pltpu.VMEM((NJ, CELLS), BF16),
            pltpu.VMEM((NJ, CELLS), BF16),
            pltpu.VMEM((CX, CY, ORB, CZ), F32),
            pltpu.VMEM((4 * ORB, CY * CZ), BF16),
            pltpu.VMEM((2 * ORB, NJ), F32),
            pltpu.VMEM((NG_Z, ORB, CZ), F32),
            pltpu.VMEM((NG_Z, ORB, CZ), F32),
            pltpu.VMEM((PLANE, ORB, CZ), F32),
            pltpu.VMEM((NG_Z, ORB, CZ), F32),
            pltpu.VMEM((2 * ORB, CELLS), F32),
            pltpu.VMEM((CX, CY, ORB, CZ), F32),
            pltpu.VMEM((CX, CY, ORB, CZ), F32),
            dma((5,)), dma((NXY,)), dma((2, 23)), dma((2, 23)), dma((12,)), dma((12,)), dma((CX,)), dma((CX,)),
            dma((NG_Z,)), dma((NG_Z,)), dma((PLANE,)), dma((PLANE,)), dma((NG_Z,)), dma((NG_Z,)),
            dma((CX,)), dma((CX,)),
        ],
        compiler_params=pltpu.CompilerParams(
            collective_id=0, has_side_effects=True, vmem_limit_bytes=60 * 1024 * 1024),
        name="filter_project",
    )(
        block.reshape(ORB * NXY, CZ), potential.reshape(NXY, CZ), proj_index, proj_value,
        proj_strength, stored.reshape(NJ, NXY, CZ))
    projected, intersection = pl.pallas_call(
        finish,
        out_shape=(jax.ShapeDtypeStruct(projected.shape, F32), jax.ShapeDtypeStruct(intersection.shape, F32)),
        in_specs=[vmem, vmem],
        out_specs=(vmem, vmem),
        name="finish",
    )(projected, intersection)
    return projected.reshape(block.shape), intersection.T


def solution(mesh):
    in_specs = (
        P("band", "gx", "gyz", None),
        P("gx", "gyz", None),
        P(("gx", "gyz"), None),
        P(("gx", "gyz"), None),
        P(("gx", "gyz")),
        P("band", "gx", "gyz", None),
    )
    out_specs = (P("band", "gx", "gyz", None), P("band", None))
    return jax.shard_map(
        on_device, mesh=mesh, in_specs=in_specs, out_specs=out_specs, check_vma=False
    )
```

time: 56.7 us -> 54.7 us (0.965)
  Pallas kernels: 55.9 us -> 54 us
    pallas_call x1, Pallas kernels: 54.3 us -> 52.4 us  [on_device(): pl.pallas_call(kernel, out_shape=(jax.ShapeDtypeStruct((ORB * NXY, CZ), F...]
where the time goes in v4:
time: 54.7 us
  Pallas kernels  54 us (99%)
  between operations  0.64 us (1%)
    pallas_call x1, Pallas kernels, on_device(): pl.pallas_call(kernel, out_shape=(jax.ShapeDtypeStruct((ORB * NXY, CZ), F...  52.4 us
    pallas_call x1, Pallas kernels, on_device(): pl.pallas_call(finish, out_shape=(jax.ShapeDtypeStruct(projected.shape, F...  1.57 us

profile of v4, /device:TPU:1, one launch (start us, length us, event | category | flops | bytes accessed | tf_op | source)
XLA Modules:
  0.0 54.7 jit_solution(10496372336901920387)
XLA Ops:
  0.6 52.4 %filter_project.1 = (f32[256,128]{1,0:T(8,128)}, f32[16,512]{1,0:T(8,128)}) custom-call(f32[256,128]{1,0:T(8,128)} %bitcast.6, f32[32,128]{1,0:T(8,128)} %bitcast.7, s32[8,128]{1,0:T(8,128)} %idx_in.1, f32[8,128]{1,0:T(8,128)} %val_in.1, f32[8]{0:T(128)} %str_in.1, f32[512,32,128]{2,1,0:T(8,128)} %bitcast.5), custom_call_target="tpu_custom_call" | custom-call | tf_op jit(solution)/shard_map/filter_project/pallas_call | solution.py:615
  53.1 1.6 %finish.1 = (f32[256,128]{1,0:T(8,128)}, f32[16,512]{1,0:T(8,128)}) custom-call(f32[256,128]{1,0:T(8,128)} %get-tuple-element.6.a_ref, f32[16,512]{1,0:T(8,128)} %get-tuple-element.7.b_ref), custom_call_target="tpu_custom_call" | custom-call | tf_op jit(solution)/shard_map/finish/pallas_call | solution.py:670

commit v5 on v4

--- a/solution.py
+++ b/solution.py
@@ -232,7 +232,7 @@
     side_scale = 0.5 / HALF
 
     def along(cur):
-        zero = jnp.zeros((1, ORB, CZ), F32)
+        zero = jnp.zeros((1,) + cur.shape[1:], F32)
         return jnp.concatenate([zero, cur[:-1]], axis=0) + jnp.concatenate([cur[1:], zero], axis=0)
 
     def along_z(cur):
@@ -306,17 +306,33 @@
         for side, at in ((0, 1), (1, 7)):
             cur = field[slot, at:at + 2, 3:11]
             near = field[slot, at - 1:at + 1, 3:11] + field[slot, at + 1:at + 3, 3:11] + along_z(cur)
-            near = near + field[slot, at:at + 2, 2:10] + field[slot, at:at + 2, 4:12]
+            near = near + jnp.stack([along(cur[0]), along(cur[1])])
             inner[at - 1:at + 1, 2:10] = (
                 beta_x[side, NPROJ] * cur - side_scale * near
                 + spread(unpack(coef_in[slot, side]), lambda p: beta_x[side, p]))
         for side, at in ((0, 1), (1, 11)):
             cur = field[slot, 3:7, at:at + 2]
             near = field[slot, 3:7, at - 1:at + 1] + field[slot, 3:7, at + 1:at + 3] + along_z(cur)
-            near = near + field[slot, 2:6, at:at + 2] + field[slot, 4:8, at:at + 2]
+            near = near + along(cur)
             inner[2:6, at - 1:at + 1] = (
                 beta_y[side, NPROJ] * cur - side_scale * near
                 + spread(unpack(coef_in[slot, 2 + side]), lambda p: beta_y[side, p]))
+    def corner_cells(slot, weights):
+        added, tiles = [], []
+        for x, y, own_x, own_y, out in ((2, 2, 3, 3, -1), (2, 11, 3, 10, 1), (7, 2, 6, 3, -1), (7, 11, 6, 10, 1)):
+            far_x, far_y = 2 * x - own_x, y + out
+            for here_x, here_y, got in ((x, own_y, (x, y)), (far_x, own_y, (far_x, y)),
+                                        (own_x, y, (x, y)), (own_x, far_y, (x, far_y))):
+                inner[here_x - 1, here_y - 1] = (
+                    inner[here_x - 1, here_y - 1] - side_scale * field[(slot,) + got])
+            more = (4.0 * side_scale * side_scale) * field[slot, x, y]
+            inner2[own_x - 2, own_y - 2] = inner2[own_x - 2, own_y - 2] + more
+            added.append(more)
+            tiles.append((own_x - 3, own_y - 3))
+        out = []
+        for p in range(NPROJ):
+            acc = sum(more * beta[p, x, y] for more, (x, y) in zip(added, tiles))
+            out.append(weights[p] + jnp.sum(acc, axis=1, keepdims=True))
         for n, (x, y) in enumerate(((2, 2), (2, 11), (7, 2), (7, 11))):
             cur = field[slot, x, y]
             near = field[slot, x - 1, y] + field[slot, x + 1, y] + field[slot, x, y - 1] + field[slot, x, y + 1]
@@ -324,39 +340,44 @@
             inner[x - 1, y - 1] = (
                 beta_d[n, NPROJ] * cur - side_scale * near
                 + spread(unpack(coef_in[slot, 4 + n]), lambda p: beta_d[n, p]))
+        return out
 
     XL, XR, YL, YR = 1, 2, 3, 4
 
     def group(tile, n):
         return pltpu.roll(tile, CZ - 8 * n, 1)
 
-    def next_coefficients(slot):
+    def next_own(slot):
+        near = [coef_in[slot, place] for place in range(4)]
+        own = group(near[0], XR) + group(near[1], XL) + group(near[2], YR) + group(near[3], YL)
+        return unpack(part[slot] - side_scale * own)
+
+    def next_around(slot):
         got = [coef_in[slot, place] for place in range(11)]
         mine = coef[slot]
-        own = group(got[0], XR) + group(got[1], XL) + group(got[2], YR) + group(got[3], YL)
         low_x = group(mine, XL) + group(got[8], XR) + group(got[4], YR) + group(got[5], YL)
         high_x = group(mine, XR) + group(got[8], XL) + group(got[6], YR) + group(got[7], YL)
         low_y = group(mine, YL) + group(got[9], YR) + group(got[4], XR) + group(got[6], XL)
         high_y = group(mine, YR) + group(got[10], YL) + group(got[5], XR) + group(got[7], XL)
-        out = [unpack(part[slot] - side_scale * own)]
-        for place, terms in enumerate((low_x, high_x, low_y, high_y)):
-            out.append(unpack(part_in[slot, place] - side_scale * terms))
-        return out
-
-    def middle(slot, weights):
+        return [unpack(part_in[slot, place] - side_scale * terms)
+                for place, terms in enumerate((low_x, high_x, low_y, high_y))]
+
+    def middle_own(slot, weights):
         for x in range(CX):
-            inner2[1 + x, 1:9] = 2.0 * own_x_of_inner(x, weights[0]) - field[slot, 3 + x, 3:11]
+            inner2[1 + x, 1:9] = 2.0 * own_x_of_inner(x, weights) - field[slot, 3 + x, 3:11]
+
+    def middle_around(slot, weights):
         for side, at in ((0, 1), (1, 6)):
             cur = inner[at, 2:10]
             near = inner[at - 1, 2:10] + inner[at + 1, 2:10] + inner[at, 1:9] + inner[at, 3:11] + along_z(cur)
             got = (beta_x[side, NPROJ, 1 - side] * cur - side_scale * near
-                   + spread(weights[1 + side], lambda p: beta_x[side, p, 1 - side]))
+                   + spread(weights[side], lambda p: beta_x[side, p, 1 - side]))
             inner2[at - 1, 1:9] = 2.0 * got - field[slot, at + 1, 3:11]
         for side, at in ((0, 1), (1, 10)):
             cur = inner[2:6, at]
             near = inner[2:6, at - 1] + inner[2:6, at + 1] + inner[1:5, at] + inner[3:7, at] + along_z(cur)
             got = (beta_y[side, NPROJ, :, 1 - side] * cur - side_scale * near
-                   + spread(weights[3 + side], lambda p: beta_y[side, p, :, 1 - side]))
+                   + spread(weights[2 + side], lambda p: beta_y[side, p, :, 1 - side]))
             inner2[1:5, at - 1] = 2.0 * got - field[slot, 3:7, at + 1]
 
     def swap(x):
@@ -364,8 +385,7 @@
             src_ref=field.at[1, 3 + x, 3:11], dst_ref=other.at[x], send_sem=bs_sem.at[x], recv_sem=br_sem.at[x],
             device_id=twin, device_id_type=MESH)
 
-    def degree_three(slot, scale, back, last):
-        weights = own_coefficients(inner2[1:5, 1:9])
+    def degree_three(slot, weights, scale, back, last):
         for x in range(CX):
             cur = inner2[1 + x, 1:9]
             near = inner2[x, 1:9] + inner2[2 + x, 1:9] + inner2[1 + x, 0:8] + inner2[1 + x, 2:10]
@@ -430,6 +450,7 @@
         tiles = coef_copies(slot, 11)
         start(tiles)
         start(faces_y)
+        start(faces_x)
 
         @pl.when(k == 0)
         def _():
@@ -442,9 +463,7 @@
             inner[2 + x, 2:10] = inside(slot, weights, x)
         part[slot] = pack(own_coefficients(inner[2:6, 2:10]))
         parts = part_copies(slot)
-        start(parts[:2])
-        start(faces_x)
-        start(parts[2:])
+        start(parts)
 
         @pl.when(k == 0)
         def _():
@@ -462,14 +481,19 @@
         def _():
             wait_sent(1)
 
-        for c in faces_x + faces_y + tuple(tiles) + tuple(parts) + corners:
+        for c in faces_x + faces_y + tuple(tiles[7:]):
             c.wait_recv()
         add_halo(slot)
         outer_layers(slot)
-        middle(slot, next_coefficients(slot))
+        middle_own(slot, next_own(slot))
+        weights = own_coefficients(inner2[1:5, 1:9])
+        for c in corners + tuple(tiles[:7]) + tuple(parts):
+            c.wait_recv()
+        weights = corner_cells(slot, weights)
+        middle_around(slot, next_around(slot))
         scale = jnp.where(k == 0, 2.0 * AT_LOW[2] / AT_LOW[5], 2.0 * AT_LOW[5] / AT_LOW[8])
         back = jnp.where(k == 0, 1.0 / AT_LOW[5], AT_LOW[2] / AT_LOW[8])
-        degree_three(slot, scale, back, k == 1)
+        degree_three(slot, weights, scale, back, k == 1)
         return carry
 
     lax.fori_loop(0, 2, step, 0)
@@ -534,7 +558,7 @@
             src_ref=g2.at[plane], dst_ref=g2.at[at], send_sem=p2s.at[i], recv_sem=p2r.at[at],
             device_id=device, device_id_type=MESH)
 
-    for i in range(1, PLANE):
+    for i in (10, 9, 11, 6, 14, 5, 7, 13, 15, 2, 8, 1, 3, 4, 12):
         send2(i).start()
     for i in range(1, NG_Z):
         recv1(i).wait_send()
@@ -547,7 +571,7 @@
             src_ref=q3.at[mz], dst_ref=q3.at[mz], send_sem=p3s.at[i], recv_sem=p3r.at[mz],
             device_id=z_peer(i)[1], device_id_type=MESH)
 
-    for i in range(1, NG_Z):
+    for i in (4, 3, 5, 2, 6, 1, 7):
         send3(i).start()
     for i in range(1, PLANE):
         send2(i).wait_send()

time: 54.7 us -> 54.5 us (level)
  no operation moved by 1% of the time
where the time goes in v5:
time: 54.5 us; the launch traced here: 54.4 us
  Pallas kernels  53.8 us (99%)
  between operations  0.64 us (1%)
    pallas_call x1, Pallas kernels, on_device(): pl.pallas_call(kernel, out_shape=(jax.ShapeDtypeStruct((ORB * NXY, CZ), F...  52.2 us
    pallas_call x1, Pallas kernels, on_device(): pl.pallas_call(finish, out_shape=(jax.ShapeDtypeStruct(projected.shape, F...  1.57 us

profile of v5, /device:TPU:1, one launch (start us, length us, event | category | flops | bytes accessed | tf_op | source)
XLA Modules:
  0.0 54.4 jit_solution(11270105161849686777)
XLA Ops:
  0.6 52.2 %filter_project.1 = (f32[256,128]{1,0:T(8,128)}, f32[16,512]{1,0:T(8,128)}) custom-call(f32[256,128]{1,0:T(8,128)} %bitcast.6, f32[32,128]{1,0:T(8,128)} %bitcast.7, s32[8,128]{1,0:T(8,128)} %idx_in.1, f32[8,128]{1,0:T(8,128)} %val_in.1, f32[8]{0:T(128)} %str_in.1, f32[512,32,128]{2,1,0:T(8,128)} %bitcast.5), custom_call_target="tpu_custom_call" | custom-call | tf_op jit(solution)/shard_map/filter_project/pallas_call | solution.py:639
  52.9 1.6 %finish.1 = (f32[256,128]{1,0:T(8,128)}, f32[16,512]{1,0:T(8,128)}) custom-call(f32[256,128]{1,0:T(8,128)} %get-tuple-element.6.a_ref, f32[16,512]{1,0:T(8,128)} %get-tuple-element.7.b_ref), custom_call_target="tpu_custom_call" | custom-call | tf_op jit(solution)/shard_map/finish/pallas_call | solution.py:694

commit v6 on v5

--- a/solution.py
+++ b/solution.py
@@ -497,13 +497,13 @@
         return carry
 
     lax.fori_loop(0, 2, step, 0)
-    wait_sent(0)
 
     first_core = band == 0
-    def send1(c):
+    def send1(i):
+        at, device = z_peer(i)
         return pltpu.make_async_remote_copy(
-            src_ref=pbuf.at[c], dst_ref=r1.at[mz], send_sem=p1s.at[c], recv_sem=p1r.at[mz],
-            device_id=(gx, c * NG_Y + my, band), device_id_type=MESH)
+            src_ref=pbuf.at[at], dst_ref=r1.at[mz], send_sem=p1s.at[at], recv_sem=p1r.at[mz],
+            device_id=device, device_id_type=MESH)
 
     nt = (((1,), (1,)), ((), ()))
     for x in range(CX):
@@ -523,17 +523,11 @@
         total[...] = got if x == 0 else total[...] + got
     for t in range(NJ // 128):
         flat = total[:, t * 128:(t + 1) * 128]
-        for h in range(2):
-            c = 2 * t + h
-            pbuf[c] = flat[8 * h:8 * h + 8]
-
-            @pl.when(mz == c)
-            def _(c=c):
-                r1[c] = pbuf[c]
-
-            @pl.when(mz != c)
-            def _(c=c):
-                send1(c).start()
+        pbuf[2 * t], pbuf[2 * t + 1] = flat[0:8], flat[8:16]
+    for i in (4, 3, 5, 2, 6, 1, 7):
+        send1(i).start()
+    r1[mz] = pbuf[mz]
+    wait_sent(0)
 
     def recv1(i):
         at, device = z_peer(i)

time: 54.5 us -> 54.5 us (level)
  no operation moved by 1% of the time
where the time goes in v6:
time: 54.5 us; the launch traced here: 54.4 us
  Pallas kernels  53.7 us (99%)
  between operations  0.64 us (1%)
    pallas_call x1, Pallas kernels, on_device(): pl.pallas_call(kernel, out_shape=(jax.ShapeDtypeStruct((ORB * NXY, CZ), F...  52.2 us
    pallas_call x1, Pallas kernels, on_device(): pl.pallas_call(finish, out_shape=(jax.ShapeDtypeStruct(projected.shape, F...  1.57 us

profile of v6, /device:TPU:1, one launch (start us, length us, event | category | flops | bytes accessed | tf_op | source)
XLA Modules:
  0.0 54.4 jit_solution(2512333406318627007)
XLA Ops:
  0.6 52.2 %filter_project.1 = (f32[256,128]{1,0:T(8,128)}, f32[16,512]{1,0:T(8,128)}) custom-call(f32[256,128]{1,0:T(8,128)} %bitcast.6, f32[32,128]{1,0:T(8,128)} %bitcast.7, s32[8,128]{1,0:T(8,128)} %idx_in.1, f32[8,128]{1,0:T(8,128)} %val_in.1, f32[8]{0:T(128)} %str_in.1, f32[512,32,128]{2,1,0:T(8,128)} %bitcast.5), custom_call_target="tpu_custom_call" | custom-call | tf_op jit(solution)/shard_map/filter_project/pallas_call | solution.py:633
  52.8 1.6 %finish.1 = (f32[256,128]{1,0:T(8,128)}, f32[16,512]{1,0:T(8,128)}) custom-call(f32[256,128]{1,0:T(8,128)} %get-tuple-element.6.a_ref, f32[16,512]{1,0:T(8,128)} %get-tuple-element.7.b_ref), custom_call_target="tpu_custom_call" | custom-call | tf_op jit(solution)/shard_map/finish/pallas_call | solution.py:688

commit v7 on v5

--- a/solution.py
+++ b/solution.py
@@ -408,13 +408,12 @@
             c.start()
 
     corners, faces_y, faces_x = halo_copies(0, 2)
-    start(corners + faces_y)
+    near_sides, next_sides, far_sides = side_copies(0), side_copies(1), diagonal_copies()
+    start(corners + near_sides[:2] + faces_y)
     weights = own_coefficients(field[0, 3:7, 3:11])
     coef[0] = pack(weights)
     tiles = coef_copies(0, 4)
     start(tiles)
-    near_sides, next_sides, far_sides = side_copies(0), side_copies(1), diagonal_copies()
-    start(near_sides[:2])
     start(faces_x)
     start(near_sides[2:])
     for x in range(CX):

time: 54.5 us -> 54.6 us (level)
  no operation moved by 1% of the time
where the time goes in v7:
time: 54.6 us; the launch traced here: 54.5 us
  Pallas kernels  53.8 us (99%)
  between operations  0.64 us (1%)
    pallas_call x1, Pallas kernels, on_device(): pl.pallas_call(kernel, out_shape=(jax.ShapeDtypeStruct((ORB * NXY, CZ), F...  52.3 us
    pallas_call x1, Pallas kernels, on_device(): pl.pallas_call(finish, out_shape=(jax.ShapeDtypeStruct(projected.shape, F...  1.57 us

profile of v7, /device:TPU:1, one launch (start us, length us, event | category | flops | bytes accessed | tf_op | source)
XLA Modules:
  0.0 54.5 jit_solution(6867408792319704894)
XLA Ops:
  0.6 52.3 %filter_project.1 = (f32[256,128]{1,0:T(8,128)}, f32[16,512]{1,0:T(8,128)}) custom-call(f32[256,128]{1,0:T(8,128)} %bitcast.6, f32[32,128]{1,0:T(8,128)} %bitcast.7, s32[8,128]{1,0:T(8,128)} %idx_in.1, f32[8,128]{1,0:T(8,128)} %val_in.1, f32[8]{0:T(128)} %str_in.1, f32[512,32,128]{2,1,0:T(8,128)} %bitcast.5), custom_call_target="tpu_custom_call" | custom-call | tf_op jit(solution)/shard_map/filter_project/pallas_call | solution.py:638
  52.9 1.6 %finish.1 = (f32[256,128]{1,0:T(8,128)}, f32[16,512]{1,0:T(8,128)}) custom-call(f32[256,128]{1,0:T(8,128)} %get-tuple-element.6.a_ref, f32[16,512]{1,0:T(8,128)} %get-tuple-element.7.b_ref), custom_call_target="tpu_custom_call" | custom-call | tf_op jit(solution)/shard_map/finish/pallas_call | solution.py:693
